TPU v7x, 512 devices: a whole 4x4x16 slice. The times are simulated.
512 devices in a mesh: row: 64 (over x, z), col: 8 (over y, core).
Axes of the slice: x: 4, y: 4, z: 16, core: 2. Of those that a mesh axis runs over, the one named last changes fastest.
Arguments:
- matrix: float32 [131072, 1024], P('row', 'col'), may hold values from -90 to 90, as said below
- row_signs: int32 [131072], P('row'), may hold values from -1 to 1, as said below
- sample_block: int32 [16384, 1], P('row'), may hold values from 0 to 63; in each aligned block of 256 rows (0 to 255, 256 to 511, ...) at most 8 rows name the same one
- sample_offset: int32 [16384], P('row'), may hold values from 0 to 2047
Outputs:
- sketch: float32 [16384, 1024], P('row', 'col')
- factor: float32 [1024, 1024], P(None, 'col')
Inputs may be any that keep to these rules, and one draw needn't show every extreme that they name: `matrix`: entries are real and of both signs; no structure is promised. `row_signs`: each entry is -1 or 1. `sample_block`: among the 256 samples of one device (aligned blocks) no value is named more than 8 times, a bound that some block reaches.
All inputs are finite; a program needn't handle non-finite values.
Results may differ from a plain program's by a relative error of at most 0.00007.
Values sent between devices are 32-bit elements; how exact they have to be, the bound alone decides.
A program may use at most 64 MiB of HBM per device.

v0:
```python
import math

import jax
import jax.numpy as jnp
from jax import lax
from jax.sharding import PartitionSpec as P

highest = lax.Precision.HIGHEST


def walsh_table(order):
    indices = jnp.arange(order, dtype=jnp.int32)
    parity = jnp.zeros((order, order), jnp.int32)
    for bitpos in range(max(order.bit_length() - 1, 0)):
        column = jnp.bitwise_and(jnp.right_shift(indices, bitpos), 1)
        parity = jnp.bitwise_xor(parity, column[:, None] * column[None, :])
    return (1 - 2 * parity).astype(jnp.float32)


def slot_numbers(blocks, devices):
    onehot = (blocks[:, None] == jnp.arange(devices, dtype=jnp.int32)[None, :]).astype(jnp.int32)
    before = jnp.cumsum(onehot, axis=0) - onehot
    return jnp.sum(before * onehot, axis=1)


def shards(matrix, row_signs, sample_block, sample_offset):
    local_rows, col_width = matrix.shape
    devices = lax.axis_size("row")
    row_block = local_rows // devices
    outer = local_rows // 64
    factor_norm = 1.0 / math.sqrt(devices * local_rows)
    signed = matrix * row_signs.astype(jnp.float32)[:, None]
    signed = signed.reshape(outer, 64, col_width)
    signed = jnp.einsum("ai,ijc->ajc", walsh_table(outer), signed, precision=highest)
    signed = jnp.einsum("bj,ajc->abc", walsh_table(64), signed, precision=highest)
    sectioned = signed.reshape(devices, row_block, col_width)
    w_cross = walsh_table(devices)
    mixed = (
        jnp.einsum(
            "qp,pic->qic",
            w_cross,
            lax.all_to_all(sectioned, "row", split_axis=0, concat_axis=0, tiled=True),
            precision=highest,
        )
        * factor_norm
    )
    holder_table = mixed.reshape(devices * row_block, col_width)
    own_count = sample_offset.shape[0]
    capacity = max(2, 2 * own_count // devices)
    blocks = sample_block[:, 0]
    slots = slot_numbers(blocks, devices)
    outgoing = jnp.zeros((devices, capacity), jnp.int32).at[blocks, slots].set(sample_offset)
    requests = lax.all_to_all(outgoing, "row", split_axis=0, concat_axis=0, tiled=True)
    answers = jnp.take(holder_table, requests.reshape(-1), axis=0).reshape(
        devices, capacity, col_width
    )
    returned = lax.all_to_all(answers, "row", split_axis=0, concat_axis=0, tiled=True)
    sketch = returned[blocks, slots]
    samples_total = own_count * devices
    panel = lax.all_gather(sketch, "col", axis=1, tiled=True)
    local_part = jnp.dot(panel.T, sketch, precision=highest, preferred_element_type=jnp.float32)
    summed = lax.psum(local_part, "row") / samples_total
    gram = lax.all_gather(summed, "col", axis=1, tiled=True)
    lower = jnp.linalg.cholesky(gram)
    return (
        sketch,
        lax.dynamic_slice_in_dim(lower, lax.axis_index("col") * col_width, col_width, 1),
    )


def solution(mesh):
    placed = (P("row", "col"), P("row"), P("row", None), P("row"))
    return jax.shard_map(
        shards,
        mesh=mesh,
        in_specs=placed,
        out_specs=(P("row", "col"), P(None, "col")),
        check_vma=False,
    )
```

profile of v0, /device:TPU:1, one launch (start us, length us, event | category | flops | bytes accessed | tf_op | source)
XLA Modules:
  0.0 715.9 jit_solution(297892763952688968)
XLA Ops:
  10.2 21.2 %scatter_fusion = s32[64,8]{0,1:T(8,128)S(1)} fusion(s32[64,8]{0,1:T(8,128)S(1)} %broadcast_in_dim.10, s32[256]{0:T(256)S(1)} %bitcast.91, s32[256]{0:T(256)} %param.7), kind=kCustom, calls=%fused_computation.2 | custom fusion | bytes 5120 | tf_op jit(solution)/shard_map/scatter | solution.py:52
  32.1 19.1 %all-to-all-start = ((s32[64,1,8]{2,1,0:T(1,128)}), s32[64,1,8]{2,1,0:T(1,128)S(1)}, u32[]{:S(2)}, u32[]{:S(2)}) async-start(s32[64,1,8]{2,1,0:T(1,128)} %copy.18), calls=%async_computation | async-start | bytes 65536 | tf_op jit(solution)/shard_map/all_to_all | solution.py:53
  55.1 2.7 fusion.3
  57.9 6.6 all-to-all-done
  64.5 8.0 %all-to-all-start.1 = ((f32[64,32,128]{2,1,0:T(8,128)}), f32[64,32,128]{2,1,0:T(8,128)S(1)}, u32[]{:S(2)}, u32[]{:S(2)}) async-start(f32[64,32,128]{2,1,0:T(8,128)} %bitcast.11), calls=%async_computation.1 | async-start | bytes 2097152 | tf_op jit(solution)/shard_map/all_to_all | solution.py:42
  74.0 48.1 %all-to-all-done.1 = f32[64,32,128]{2,1,0:T(8,128)S(1)} async-done(((f32[64,32,128]{2,1,0:T(8,128)}), f32[64,32,128]{2,1,0:T(8,128)S(1)}, u32[]{:S(2)}, u32[]{:S(2)}) %all-to-all-start.1) | async-done | bytes 1048608 | tf_op jit(solution)/shard_map/all_to_all | solution.py:42
  125.6 29.1 %all_to_all.19 = f32[64,8,128]{2,1,0:T(8,128)S(1)} all-to-all(f32[64,8,128]{2,1,0:T(8,128)S(1)} %bitcast_select_fusion), channel_id=1, replica_groups=mesh['row'=64,'col'=8] {'row'}, dimensions={0} | all-to-all | bytes 524288 | tf_op jit(solution)/shard_map/all_to_all | solution.py:57
  156.8 26.5 %all-gather.3.cloned.1.call-done = f32[256,1024]{1,0:T(8,128)} async-done(((f32[256,128]{1,0:T(8,128)}), f32[256,1024]{1,0:T(8,128)}) %all-gather.3.cloned.1.call-update) | async-done | bytes 1048592 | tf_op jit(solution)/shard_map/all_gather | solution.py:60
  183.4 2.8 fusion.103
  186.2 257.7 %all-reduce.3.cloned.1.call-done = f32[1024,128]{0,1:T(8,128)} async-done(((f32[1024,128]{0,1:T(8,128)}), f32[1024,128]{0,1:T(8,128)}) %all-reduce.3.cloned.1.call-update) | async-done | bytes 524304 | tf_op jit(solution)/shard_map/psum | solution.py:62
  445.8 45.7 %all-gather.5.cloned.1.call-done = f32[1024,1024]{0,1:T(8,128)} async-done(((f32[1024,128]{0,1:T(8,128)}), f32[1024,1024]{0,1:T(8,128)}) %all-gather.5.cloned.1.call-update) | async-done | bytes 4194320 | tf_op jit(solution)/shard_map/all_gather | solution.py:63
  491.5 5.8 copy.26
  497.3 4.4 fusion
  503.7 11.7 %cholesky.223 = f32[128,128]{1,0:T(8,128)S(1)} custom-call(f32[128,128]{1,0:T(8,128)S(1)} %cholesky.580), custom_call_target="Cholesky" | custom-call | tf_op jit(solution)/shard_map/jit(cholesky)/cholesky | solution.py:64
  515.4 2.5 cholesky.255
  517.9 9.8 %custom-call.59 = f32[1,128,128]{1,2,0:T(8,128)S(1)} custom-call(f32[1,128,128]{2,1,0:T(8,128)S(1)} %get-tuple-element.25), custom_call_target="InvertDiagBlocksLowerTriangular" | custom-call | tf_op jit(solution)/shard_map/jit(cholesky)/cholesky | solution.py:64
  527.7 2.4 constant_dynamic-update-slice_fusion.7
  531.7 11.9 %cholesky.244 = f32[128,128]{1,0:T(8,128)S(1)} custom-call(f32[128,128]{1,0:T(8,128)S(1)} %cholesky.584), custom_call_target="Cholesky" | custom-call | tf_op jit(solution)/shard_map/jit(cholesky)/cholesky | solution.py:64
  545.4 9.8 %custom-call.60 = f32[1,128,128]{1,2,0:T(8,128)S(1)} custom-call(f32[1,128,128]{2,1,0:T(8,128)S(1)} %get-tuple-element.22), custom_call_target="InvertDiagBlocksLowerTriangular" | custom-call | tf_op jit(solution)/shard_map/jit(cholesky)/cholesky | solution.py:64
  558.6 11.7 %cholesky.468 = f32[128,128]{1,0:T(8,128)S(1)} custom-call(f32[128,128]{1,0:T(8,128)S(1)} %cholesky.589), custom_call_target="Cholesky" | custom-call | tf_op jit(solution)/shard_map/jit(cholesky)/cholesky | solution.py:64
  571.6 9.8 %custom-call.61 = f32[1,128,128]{1,2,0:T(8,128)S(1)} custom-call(f32[1,128,128]{2,1,0:T(8,128)S(1)} %get-tuple-element.19), custom_call_target="InvertDiagBlocksLowerTriangular" | custom-call | tf_op jit(solution)/shard_map/jit(cholesky)/cholesky | solution.py:64
  582.6 2.3 convolution_subtract_fusion.2
  584.9 11.9 %cholesky.487 = f32[128,128]{1,0:T(8,128)S(1)} custom-call(f32[128,128]{1,0:T(8,128)S(1)} %cholesky.594), custom_call_target="Cholesky" | custom-call | tf_op jit(solution)/shard_map/jit(cholesky)/cholesky | solution.py:64
  598.1 9.8 %custom-call.62 = f32[1,128,128]{1,2,0:T(8,128)S(1)} custom-call(f32[1,128,128]{2,1,0:T(8,128)S(1)} %get-tuple-element.16), custom_call_target="InvertDiagBlocksLowerTriangular" | custom-call | tf_op jit(solution)/shard_map/jit(cholesky)/cholesky | solution.py:64
  609.0 2.3 convolution_subtract_fusion.3
  611.4 11.7 %cholesky.506 = f32[128,128]{1,0:T(8,128)S(1)} custom-call(f32[128,128]{1,0:T(8,128)S(1)} %cholesky.599), custom_call_target="Cholesky" | custom-call | tf_op jit(solution)/shard_map/jit(cholesky)/cholesky | solution.py:64
  624.4 10.2 %custom-call.63 = f32[1,128,128]{1,2,0:T(8,128)S(1)} custom-call(f32[1,128,128]{2,1,0:T(8,128)S(1)} %get-tuple-element.13), custom_call_target="InvertDiagBlocksLowerTriangular" | custom-call | tf_op jit(solution)/shard_map/jit(cholesky)/cholesky | solution.py:64
  637.9 11.7 %cholesky.526 = f32[128,128]{1,0:T(8,128)S(1)} custom-call(f32[128,128]{1,0:T(8,128)S(1)} %cholesky.604), custom_call_target="Cholesky" | custom-call | tf_op jit(solution)/shard_map/jit(cholesky)/cholesky | solution.py:64
  650.8 9.8 %custom-call.64 = f32[1,128,128]{1,2,0:T(8,128)S(1)} custom-call(f32[1,128,128]{2,1,0:T(8,128)S(1)} %get-tuple-element.10), custom_call_target="InvertDiagBlocksLowerTriangular" | custom-call | tf_op jit(solution)/shard_map/jit(cholesky)/cholesky | solution.py:64
  663.6 11.9 %cholesky.546 = f32[128,128]{1,0:T(8,128)S(1)} custom-call(f32[128,128]{1,0:T(8,128)S(1)} %cholesky.609), custom_call_target="Cholesky" | custom-call | tf_op jit(solution)/shard_map/jit(cholesky)/cholesky | solution.py:64
  676.8 9.8 %custom-call.65 = f32[1,128,128]{1,2,0:T(8,128)S(1)} custom-call(f32[1,128,128]{2,1,0:T(8,128)S(1)} %get-tuple-element.7), custom_call_target="InvertDiagBlocksLowerTriangular" | custom-call | tf_op jit(solution)/shard_map/jit(cholesky)/cholesky | solution.py:64
  689.3 11.7 %cholesky.564 = f32[128,128]{1,0:T(8,128)S(1)} custom-call(f32[128,128]{1,0:T(8,128)S(1)} %convolution_subtract_fusion.6), custom_call_target="Cholesky" | custom-call | tf_op jit(solution)/shard_map/jit(cholesky)/cholesky | solution.py:64
  (75 shorter events, 46.2 us)
Async XLA Ops:
  32.1 32.3 %all-to-all-start = ((s32[64,1,8]{2,1,0:T(1,128)}), s32[64,1,8]{2,1,0:T(1,128)S(1)}, u32[]{:S(2)}, u32[]{:S(2)}) async-start(s32[64,1,8]{2,1,0:T(1,128)} %copy.18), calls=%async_computation | async-start | bytes 65536 | tf_op jit(solution)/shard_map/all_to_all | solution.py:53
  64.5 57.7 %all-to-all-start.1 = ((f32[64,32,128]{2,1,0:T(8,128)}), f32[64,32,128]{2,1,0:T(8,128)S(1)}, u32[]{:S(2)}, u32[]{:S(2)}) async-start(f32[64,32,128]{2,1,0:T(8,128)} %bitcast.11), calls=%async_computation.1 | async-start | bytes 2097152 | tf_op jit(solution)/shard_map/all_to_all | solution.py:42
  72.4 110.9 %all-gather.3.cloned.1.call-start = ((), (), s32[]{:S(2)}) async-start(), calls=%async_computation.3 | async-start | bytes 1179648 | tf_op jit(solution)/shard_map/all_gather | solution.py:60
  156.8 287.1 %all-reduce.3.cloned.1.call-start = ((), (), s32[]{:S(2)}) async-start(), calls=%async_computation.4 | async-start | bytes 1048576 | tf_op jit(solution)/shard_map/psum | solution.py:62
  186.1 305.4 %all-gather.5.cloned.1.call-start = ((), (), s32[]{:S(2)}) async-start(), calls=%async_computation.5 | async-start | bytes 4718592 | tf_op jit(solution)/shard_map/all_gather | solution.py:63
  501.7 1.9 copy-start
Sparse Core Ops, SparseCore 0:
  156.9 26.4 all-gather.2
  187.4 256.4 all-reduce.2
  446.8 44.6 all-gather.4
where the time goes:
time: 726 us; the launch traced here: 716 us
  waiting for transfers between devices  385 us (53%)
  other arithmetic  187 us (26%)
  local copies, waits for them, and re-layouts  36.8 us (5%)
  matrix products  31.7 us (4%)
  blocking collectives  29.1 us (4%)
  starting transfers between devices  27.2 us (4%)
  between operations  19.2 us (3%)
    psum x1, waiting for transfers between devices, shards(): summed = lax.psum(local_part, 'row') / samples_total  258 us
    another operation x31, other arithmetic, shards(): lower = jnp.linalg.cholesky(gram)  173 us
    all_to_all x1, waiting for transfers between devices, shards(): lax.all_to_all(sectioned, 'row', split_axis=0, concat_axis=0, tiled=True)  48.1 us
    all_gather x1, waiting for transfers between devices, shards(): gram = lax.all_gather(summed, 'col', axis=1, tiled=True)  45.7 us
    all_to_all x1, blocking collectives, shards(): lax.all_to_all(answers, 'row', split_axis=0, concat_axis=0, tiled=True)  29.1 us
    all_gather x1, waiting for transfers between devices, shards(): panel = lax.all_gather(sketch, 'col', axis=1, tiled=True)  26.5 us
    another operation x14, matrix products, shards(): lower = jnp.linalg.cholesky(gram)  23.1 us
    scatter x1, local copies, waits for them, and re-layouts, shards(): jnp.zeros((devices, capacity), jnp.int32).at[blocks, slots]  21.2 us
  transfers between devices with their start and end apart: 5, of which 5 were waited for; matrix products, arithmetic and copies ran while one was open for 1% of the time, Pallas kernels for 0%

commit v1 on v0

--- a/solution.py
+++ b/solution.py
@@ -1,8 +1,11 @@
+import functools
 import math
 
 import jax
 import jax.numpy as jnp
 from jax import lax
+from jax.experimental import pallas as pl
+from jax.experimental.pallas import tpu as pltpu
 from jax.sharding import PartitionSpec as P
 
 highest = lax.Precision.HIGHEST
@@ -15,6 +18,101 @@
         column = jnp.bitwise_and(jnp.right_shift(indices, bitpos), 1)
         parity = jnp.bitwise_xor(parity, column[:, None] * column[None, :])
     return (1 - 2 * parity).astype(jnp.float32)
+
+
+f32, bf16 = jnp.float32, jnp.bfloat16
+TN = (((0,), (0,)), ((), ()))
+PAN = 128
+BLK = 16
+
+
+def panel_factor(aug, upan):
+    cur = aug[0:BLK, :]
+    nblk = PAN // BLK
+    for t in range(nblk):
+        lo = t * BLK
+        last = t == nblk - 1
+        x = cur[:, lo:lo + BLK]
+        C = [jnp.broadcast_to(x[:, k:k + 1], (BLK, PAN)) for k in range(BLK)]
+        R = [cur[:, 0:PAN], cur[:, PAN:2 * PAN]]
+        if not last:
+            xt = jnp.transpose(cur[:, 0:PAN])[lo + BLK:lo + 2 * BLK, :]
+            N = [jnp.broadcast_to(xt[:, k:k + 1], (BLK, PAN)) for k in range(BLK)]
+            nxt = aug[lo + BLK:lo + 2 * BLK, :]
+            if t > 0:
+                done = upan[0:lo, :]
+                nxt = nxt - lax.dot_general(done[:, lo + BLK:lo + 2 * BLK], done, TN,
+                                            precision=lax.Precision.HIGHEST, preferred_element_type=f32)
+            Rn = [nxt[:, 0:PAN], nxt[:, PAN:2 * PAN]]
+        for k in range(BLK):
+            rs = lax.rsqrt(C[k][k:k + 1, :])
+            u = [R[h][k:k + 1, :] * rs for h in range(2)]
+            for h in range(2):
+                upan[lo + k:lo + k + 1, h * PAN:(h + 1) * PAN] = u[h]
+            L = C[k] * rs
+            if not last:
+                Nl = N[k] * rs
+            for c in range(k + 1, BLK):
+                m = L[c:c + 1, :]
+                if c < 8:
+                    C[c] = C[c] - L * m
+                else:
+                    C[c] = C[c] - L * m
+                if not last:
+                    N[c] = N[c] - Nl * m
+            for h in range(2):
+                if k < BLK - 1:
+                    R[h] = R[h] - L * u[h]
+                if not last:
+                    Rn[h] = Rn[h] - Nl * u[h]
+        if not last:
+            cur = jnp.concatenate(Rn, axis=1)
+
+
+def chol_kernel(n, g_ref, out_ref, s, u, aug, upan):
+    np_ = n // PAN
+    s[...] = g_ref[...]
+    u[...] = jnp.zeros_like(u)
+    ri = lax.broadcasted_iota(jnp.int32, (PAN, PAN), 0)
+    ci = lax.broadcasted_iota(jnp.int32, (PAN, PAN), 1)
+
+    def body(p, _):
+        base = pl.multiple_of(p * PAN, PAN)
+        aug[:, 0:PAN] = s[pl.ds(base, PAN), pl.ds(base, PAN)]
+        aug[:, PAN:] = jnp.where(ri == ci, 1.0, 0.0).astype(f32)
+        panel_factor(aug, upan)
+        u[pl.ds(base, PAN), pl.ds(base, PAN)] = jnp.where(ri <= ci, upan[:, 0:PAN], 0.0)
+        for pp in range(np_ - 1):
+            @pl.when(p == pp)
+            def _():
+                a0, a1, rest = pp * PAN, (pp + 1) * PAN, n
+                linv = jnp.where(ri >= ci, upan[:, PAN:], 0.0)
+                w = lax.dot_general(linv, s[a0:a1, a1:], (((1,), (0,)), ((), ())),
+                                    precision=lax.Precision.HIGHEST, preferred_element_type=f32)
+                u[a0:a1, a1:] = w
+                for q in range(pp + 1, np_):
+                    q0 = q * PAN
+                    s[q0:q0 + PAN, q0:] = s[q0:q0 + PAN, q0:] - lax.dot_general(
+                        w[:, q0 - a1:q0 - a1 + PAN], w[:, q0 - a1:], TN,
+                        precision=lax.Precision.HIGHEST, preferred_element_type=f32)
+        return 0
+
+    lax.fori_loop(0, np_, body, 0)
+    out_ref[...] = u[...]
+
+
+def chol(g):
+    n = g.shape[0]
+    return pl.pallas_call(
+        functools.partial(chol_kernel, n),
+        out_shape=jax.ShapeDtypeStruct((n, n), f32),
+        in_specs=[pl.BlockSpec(memory_space=pltpu.VMEM)],
+        out_specs=pl.BlockSpec(memory_space=pltpu.VMEM),
+        scratch_shapes=[pltpu.VMEM((n, n), f32), pltpu.VMEM((n, n), f32),
+                        pltpu.VMEM((PAN, 2 * PAN), f32), pltpu.VMEM((PAN, 2 * PAN), f32)],
+        compiler_params=pltpu.CompilerParams(vmem_limit_bytes=48 * 2**20),
+        name="chol",
+    )(g)
 
 
 def slot_numbers(blocks, devices):
@@ -59,13 +157,13 @@
     samples_total = own_count * devices
     panel = lax.all_gather(sketch, "col", axis=1, tiled=True)
     local_part = jnp.dot(panel.T, sketch, precision=highest, preferred_element_type=jnp.float32)
-    summed = lax.psum(local_part, "row") / samples_total
-    gram = lax.all_gather(summed, "col", axis=1, tiled=True)
-    lower = jnp.linalg.cholesky(gram)
-    return (
-        sketch,
-        lax.dynamic_slice_in_dim(lower, lax.axis_index("col") * col_width, col_width, 1),
-    )
+    pieces = local_part.reshape(devices, -1, col_width)
+    pieces = lax.all_to_all(pieces, "row", split_axis=0, concat_axis=0, tiled=True)
+    summed = jnp.sum(pieces, axis=0) / samples_total
+    gram = lax.all_gather(lax.all_gather(summed, "col", axis=1, tiled=True), "row", axis=0, tiled=True)
+    upper = chol(gram)
+    own = lax.dynamic_slice_in_dim(upper, lax.axis_index("col") * col_width, col_width, 0)
+    return sketch, own.T
 
 
 def solution(mesh):

time: 726 us -> 428 us (0.59)
  other arithmetic: 187 us -> 6.04 us
  waiting for transfers between devices: 385 us -> 211 us
  blocking collectives: 29.1 us -> 90.9 us
  Pallas kernels: 0 us -> 34.1 us
  matrix products: 31.7 us -> 8.92 us
  local copies, waits for them, and re-layouts: 36.8 us -> 27.6 us
    psum x1 -> x0, waiting for transfers between devices: 258 us -> none  [shards(): summed = lax.psum(local_part, 'row') / samples_total]
    another operation x33 -> x2, other arithmetic: 174 us -> 0.64 us  [the longest x31 173 us: shards(): lower = jnp.linalg.cholesky(gram)]
    all_gather x1, waiting for transfers between devices: 45.7 us -> 129 us  [shards(): lax.all_gather(lax.all_gather(summed, 'col', axis=1, tiled=True), 'row',...]
    all_to_all x0 -> x1, blocking collectives: none -> 45.1 us  [shards(): lax.all_to_all(pieces, 'row', split_axis=0, concat_axis=0, tiled=True)]
    pallas_call x0 -> x1, Pallas kernels: none -> 34.1 us  [chol(): pl.pallas_call(functools.partial(chol_kernel, n), out_shape=jax.ShapeDtyp...]
    another operation x14 -> x0, matrix products: 23.1 us -> none  [shards(): lower = jnp.linalg.cholesky(gram)]
    all_gather x0 -> x1, blocking collectives: none -> 16.6 us  [shards(): lax.all_gather(summed, 'col', axis=1, tiled=True)]
  transfers between devices with their start and end apart: 5 -> 4, of which waited for: 5 -> 4; matrix products, arithmetic and copies ran while one was open for 1% -> 2% of each run, Pallas kernels for 0% -> 0%
where the time goes in v1:
time: 428 us; the launch traced here: 420 us
  waiting for transfers between devices  211 us (49%)
  blocking collectives  90.9 us (21%)
  Pallas kernels  34.1 us (8%)
  local copies, waits for them, and re-layouts  27.6 us (6%)
  starting transfers between devices  27.4 us (6%)
  between operations  14.2 us (3%)
  matrix products  8.92 us (2%)
  other arithmetic  6.04 us (1%)
    all_gather x1, waiting for transfers between devices, shards(): lax.all_gather(lax.all_gather(summed, 'col', axis=1, tiled=True), 'row',...  129 us
    all_to_all x1, waiting for transfers between devices, shards(): lax.all_to_all(sectioned, 'row', split_axis=0, concat_axis=0, tiled=True)  48.1 us
    all_to_all x1, blocking collectives, shards(): lax.all_to_all(pieces, 'row', split_axis=0, concat_axis=0, tiled=True)  45.1 us
    pallas_call x1, Pallas kernels, chol(): pl.pallas_call(functools.partial(chol_kernel, n), out_shape=jax.ShapeDtyp...  34.1 us
    all_to_all x1, blocking collectives, shards(): lax.all_to_all(answers, 'row', split_axis=0, concat_axis=0, tiled=True)  29.1 us
    all_gather x1, waiting for transfers between devices, shards(): panel = lax.all_gather(sketch, 'col', axis=1, tiled=True)  26.4 us
    scatter x1, local copies, waits for them, and re-layouts, shards(): jnp.zeros((devices, capacity), jnp.int32).at[blocks, slots]  21.2 us
    all_to_all x1, starting transfers between devices, shards(): lax.all_to_all(outgoing, 'row', split_axis=0, concat_axis=0, tiled=True)  19.1 us
  transfers between devices with their start and end apart: 4, of which 4 were waited for; matrix products, arithmetic and copies ran while one was open for 2% of the time, Pallas kernels for 0%

profile of v1, /device:TPU:1, one launch (start us, length us, event | category | flops | bytes accessed | tf_op | source)
XLA Modules:
  0.0 419.7 jit_solution(2619497366324520677)
XLA Ops:
  7.2 0.7 fusion.8
  7.9 0.6 reduce-window.6
  8.5 0.2 slice_reduce_fusion
  8.7 0.8 fusion.7
  9.5 0.7 or_select_fusion
  10.2 21.2 %scatter_fusion = s32[64,8]{0,1:T(8,128)S(1)} fusion(s32[64,8]{0,1:T(8,128)S(1)} %broadcast_in_dim.9, s32[256]{0:T(256)S(1)} %bitcast.52, s32[256]{0:T(256)} %param.7), kind=kCustom, calls=%fused_computation.2 | custom fusion | bytes 5120 | tf_op jit(solution)/shard_map/scatter | solution.py:150
  31.4 0.7 copy.16
  32.1 19.1 %all-to-all-start = ((s32[64,1,8]{2,1,0:T(1,128)}), s32[64,1,8]{2,1,0:T(1,128)S(1)}, u32[]{:S(2)}, u32[]{:S(2)}) async-start(s32[64,1,8]{2,1,0:T(1,128)} %copy.16), calls=%async_computation | async-start | bytes 65536 | tf_op jit(solution)/shard_map/all_to_all | solution.py:151
  51.3 0.7 convert_element_type.23
  52.0 1.6 broadcast_multiply_fusion
  53.6 1.6 fusion.3
  55.2 2.7 fusion.1
  57.9 6.6 %all-to-all-done = s32[64,1,8]{2,1,0:T(1,128)S(1)} async-done(((s32[64,1,8]{2,1,0:T(1,128)}), s32[64,1,8]{2,1,0:T(1,128)S(1)}, u32[]{:S(2)}, u32[]{:S(2)}) %all-to-all-start) | async-done | bytes 2080 | tf_op jit(solution)/shard_map/all_to_all | solution.py:151
  64.5 8.0 %all-to-all-start.1 = ((f32[64,32,128]{2,1,0:T(8,128)}), f32[64,32,128]{2,1,0:T(8,128)S(1)}, u32[]{:S(2)}, u32[]{:S(2)}) async-start(f32[64,32,128]{2,1,0:T(8,128)} %bitcast.11), calls=%async_computation.1 | async-start | bytes 2097152 | tf_op jit(solution)/shard_map/all_to_all | solution.py:140
  72.5 0.5 broadcast.388
  73.0 0.7 reduce.5
  73.9 0.1 copy.18
  74.0 48.1 %all-to-all-done.1 = f32[64,32,128]{2,1,0:T(8,128)S(1)} async-done(((f32[64,32,128]{2,1,0:T(8,128)}), f32[64,32,128]{2,1,0:T(8,128)S(1)}, u32[]{:S(2)}, u32[]{:S(2)}) %all-to-all-start.1) | async-done | bytes 1048608 | tf_op jit(solution)/shard_map/all_to_all | solution.py:140
  122.2 1.6 convolution_multiply_fusion
  123.8 0.6 copy.22
  124.4 1.0 gather_fusion
  125.5 0.1 bitcast_select_fusion
  125.6 29.1 %all_to_all.24 = f32[64,8,128]{2,1,0:T(8,128)S(1)} all-to-all(f32[64,8,128]{2,1,0:T(8,128)S(1)} %bitcast_select_fusion), channel_id=1, replica_groups=mesh['row'=64,'col'=8] {'row'}, dimensions={0} | all-to-all | bytes 524288 | tf_op jit(solution)/shard_map/all_to_all | solution.py:155
  154.7 2.0 gather_fusion.1
  156.8 0.2 all-gather.5.cloned.1.call-start
  157.0 26.4 %all-gather.3.cloned.1.call-done = f32[256,1024]{1,0:T(8,128)} async-done(((f32[256,128]{1,0:T(8,128)}), f32[256,1024]{1,0:T(8,128)}) %all-gather.3.cloned.1.call-update) | async-done | bytes 1048592 | tf_op jit(solution)/shard_map/all_gather | solution.py:158
  183.4 3.0 fusion.74
  186.4 45.1 %all_to_all.25 = f32[64,16,128]{2,1,0:T(8,128)S(1)} all-to-all(f32[64,16,128]{2,1,0:T(8,128)S(1)} %bitcast.55), channel_id=1, replica_groups=mesh['row'=64,'col'=8] {'row'}, dimensions={0} | all-to-all | bytes 1048576 | tf_op jit(solution)/shard_map/all_to_all | solution.py:161
  231.6 16.6 %all_gather.10 = f32[16,1024]{1,0:T(8,128)} all-gather(f32[16,128]{1,0:T(8,128)S(1)} %broadcast_multiply_fusion.1), channel_id=1, replica_groups=mesh['row'=64,'col'=8] {'col'}, dimensions={1}, use_global_device_ids=true | all-gather | bytes 73728 | tf_op jit(solution)/shard_map/all_gather | solution.py:163
  248.3 129.5 %all-gather.5.cloned.1.call-done.g_ref = f32[1024,1024]{1,0:T(8,128)} async-done(((f32[16,1024]{1,0:T(8,128)}), f32[1024,1024]{1,0:T(8,128)}) %all-gather.5.cloned.1.call-update) | async-done | bytes 4194320 | tf_op jit(solution)/shard_map/all_gather | solution.py:163
  377.7 34.1 %chol.1 = f32[1024,1024]{1,0:T(8,128)S(1)} custom-call(f32[1024,1024]{1,0:T(8,128)} %all-gather.5.cloned.1.call-done.g_ref), custom_call_target="tpu_custom_call" | custom-call | tf_op jit(solution)/shard_map/chol/pallas_call | solution.py:106
  411.9 1.0 copy.23
  (20 shorter events, 0.4 us)
Async XLA Ops:
  32.1 32.3 %all-to-all-start = ((s32[64,1,8]{2,1,0:T(1,128)}), s32[64,1,8]{2,1,0:T(1,128)S(1)}, u32[]{:S(2)}, u32[]{:S(2)}) async-start(s32[64,1,8]{2,1,0:T(1,128)} %copy.16), calls=%async_computation | async-start | bytes 65536 | tf_op jit(solution)/shard_map/all_to_all | solution.py:151
  64.5 57.7 %all-to-all-start.1 = ((f32[64,32,128]{2,1,0:T(8,128)}), f32[64,32,128]{2,1,0:T(8,128)S(1)}, u32[]{:S(2)}, u32[]{:S(2)}) async-start(f32[64,32,128]{2,1,0:T(8,128)} %bitcast.11), calls=%async_computation.1 | async-start | bytes 2097152 | tf_op jit(solution)/shard_map/all_to_all | solution.py:140
  72.4 110.9 %all-gather.3.cloned.1.call-start = ((), (), s32[]{:S(2)}) async-start(), calls=%async_computation.4 | async-start | bytes 1179648 | tf_op jit(solution)/shard_map/all_gather | solution.py:158
  156.8 220.9 %all-gather.5.cloned.1.call-start = ((), (), s32[]{:S(2)}) async-start(), calls=%async_computation.5 | async-start | bytes 4259840 | tf_op jit(solution)/shard_map/all_gather | solution.py:163
Sparse Core Ops, SparseCore 0:
  156.9 26.4 all-gather.2
  248.4 129.2 all-gather.4

commit v2 on v1

v2 whole, which is shorter than its diff:
```python
import functools
import math

import jax
import jax.numpy as jnp
from jax import lax
from jax.experimental import pallas as pl
from jax.experimental.pallas import tpu as pltpu
from jax.sharding import PartitionSpec as P

f32, bf16 = jnp.float32, jnp.bfloat16
TN = (((0,), (0,)), ((), ()))
HI = lax.Precision.HIGHEST


def butterflies(v):
    n, step = len(v), 1
    while step < n:
        v = [v[i] + v[i + step] if not i & step else v[i - step] - v[i] for i in range(n)]
        step *= 2
    return v


def mix_pass(src, dst, rows, low, bits, scale=None):
    n, stride = 1 << bits, 1 << low
    tiles = stride // 8
    groups = rows // (n * stride)

    def body(t, _):
        g, j = t // tiles, t % tiles
        base = g * (n * stride) + j * 8
        v = [src[pl.ds(pl.multiple_of(base + i * stride, 8), 8), :] for i in range(n)]
        v = butterflies(v)
        for i in range(n):
            dst[pl.ds(pl.multiple_of(base + i * stride, 8), 8), :] = v[i] if scale is None else v[i] * scale
        return 0

    lax.fori_loop(0, groups * tiles, body, 0, unroll=2 if groups * tiles % 2 == 0 else 1)


def exchange_kernel(X, Z, C, norm, samples,
                    a_ref, sign_ref, blk_ref, off_ref,
                    gram_ref, sk_ref,
                    v, recv, table, req, reqr, reqs, own, owns, ans, ret, xall, part, xr, zs, zr, xg,
                    s_req, r_req, s_sec, r_sec, s_ans, r_ans, s_col, r_col, s_x, r_x, s_z, r_z,
                    s_zg, r_zg, s_xg, r_xg, s_cg, r_cg, l_sem):
    D = X * Z
    rows = a_ref.shape[0]
    rb = rows // D
    W = a_ref.shape[1]
    cap = ans.shape[0] // D
    S = blk_ref.shape[0]
    me, col = lax.axis_index("row"), lax.axis_index("col")
    mx, mz = me // Z, me % Z
    sib = col + 1 - 2 * (col % 2)

    def rcopy(src, dst, ss, rs, row=None, c=None):
        dev = {"row": row} if c is None else {"col": c}
        return pltpu.make_async_remote_copy(src_ref=src, dst_ref=dst, send_sem=ss, recv_sem=rs,
                                            device_id=dev, device_id_type=pl.DeviceIdType.MESH)

    bar = pltpu.get_barrier_semaphore()

    def greet(k, _):
        pl.semaphore_signal(bar, inc=1, device_id={"row": lax.rem(me + k, D)}, device_id_type=pl.DeviceIdType.MESH)
        return 0
    lax.fori_loop(1, D, greet, 0)
    ypeers = [lax.rem(col + 2 * k, C) for k in range(1, C // 2)]
    for c in [sib] + ypeers:
        pl.semaphore_signal(bar, inc=1, device_id={"col": c}, device_id_type=pl.DeviceIdType.MESH)

    blocks = blk_ref[...]
    lane = lax.broadcasted_iota(jnp.int32, (S, 128), 1)
    onehot = (blocks == lane).astype(f32)
    ri = lax.broadcasted_iota(jnp.int32, (S, S), 0)
    ci = lax.broadcasted_iota(jnp.int32, (S, S), 1)
    before = jnp.dot((ci < ri).astype(bf16), onehot.astype(bf16), preferred_element_type=f32)
    slot = jnp.sum(before * onehot, axis=1, keepdims=True)
    offs = jnp.transpose(jnp.concatenate(
        [off_ref[...].astype(f32), jnp.zeros((128 - S // 128, 128), f32)], axis=0))
    offc = jnp.concatenate([offs[:, k:k + 1] for k in range(S // 128)], axis=0)
    val = jnp.where(lane.astype(f32) == slot, offc - float(rows), 0.0)
    wanted = lax.dot_general(onehot, val, TN, precision=HI, preferred_element_type=f32) + float(rows)
    wanted = wanted.astype(jnp.int32)
    for j in range(D):
        req[j] = wanted[j:j + 1, :]
    place = (blocks.astype(f32) * float(cap) + slot)
    for k in range(S // 128):
        t = jnp.transpose(jnp.broadcast_to(place[k * 128:(k + 1) * 128, :], (128, 128)))
        own[k] = t[0:1, :].astype(jnp.int32)
    oc = pltpu.make_async_copy(own, owns, l_sem.at[0])
    oc.start()

    nb = rows // 128
    st = jnp.transpose(jnp.concatenate([sign_ref[...].astype(f32), jnp.zeros((128 - nb, 128), f32)], axis=0))
    for j in range(nb):
        v[j * 128:(j + 1) * 128, :] = a_ref[j * 128:(j + 1) * 128, :] * jnp.broadcast_to(st[:, j:j + 1], (128, W))

    def low_bits(g, _):
        base = pl.multiple_of(g * 64, 64)
        w = butterflies([v[pl.ds(base + k, 8, stride=8), :] for k in range(8)])
        for k in range(8):
            v[pl.ds(base + k, 8, stride=8), :] = w[k]
        return 0
    lax.fori_loop(0, rows // 64, low_bits, 0, unroll=2)
    left, low = rows.bit_length() - 1 - 3, 3
    while left:
        b = min(3, left)
        mix_pass(v, v, rows, low, b)
        low, left = low + b, left - b

    pl.semaphore_wait(bar, D - 1 + 1 + len(ypeers))

    def peer_of(k):
        return lax.rem(me + jnp.where(k % 2 == 1, (k + 1) // 2, D - k // 2), D)

    def sends(fn):
        def go(k, _):
            fn(peer_of(k)).start()
            return 0
        lax.fori_loop(1, D, go, 0)

    def waits(fn, recv_side):
        def go(k, _):
            c = fn(lax.rem(me + k, D))
            if recv_side:
                c.wait_recv()
            else:
                c.wait_send()
            return 0
        lax.fori_loop(1, D, go, 0)

    c_req = lambda j: rcopy(req.at[j], reqr.at[me], s_req.at[j], r_req.at[me], row=j)
    w_req = lambda j: rcopy(req.at[j], reqr.at[j], s_req.at[j], r_req.at[j], row=j)
    sec = lambda j: v.at[pl.ds(pl.multiple_of(j * rb, rb), rb), :]
    got = lambda j: recv.at[pl.ds(pl.multiple_of(j * rb, rb), rb), :]
    c_sec = lambda j: rcopy(sec(j), got(me), s_sec.at[j], r_sec.at[me], row=j)
    w_sec = lambda j: rcopy(sec(j), got(j), s_sec.at[j], r_sec.at[j], row=j)
    sends(c_req)
    sends(c_sec)
    reqr[me] = req[me]
    recv[pl.ds(pl.multiple_of(me * rb, rb), rb), :] = v[pl.ds(pl.multiple_of(me * rb, rb), rb), :]
    table[rows:rows + 8, :] = jnp.zeros((8, W), f32)
    waits(w_req, True)
    rc = pltpu.make_async_copy(reqr, reqs, l_sem.at[1])
    rc.start()
    rc.wait()
    oc.wait()
    waits(w_sec, True)

    lowb = rb.bit_length() - 1
    left, low, first = D.bit_length() - 1, lowb, True
    while left:
        b = min(3, left)
        left -= b
        mix_pass(recv if first else table, table, rows, low, b, norm if left == 0 else None)
        low, first = low + b, False

    def answer(j, _):
        for c in range(cap):
            ans[pl.ds(j * cap + c, 1), :] = table[pl.ds(jnp.clip(reqs[j, 0, c], 0, rows), 1), :]
        return 0
    lax.fori_loop(0, D, answer, 0, unroll=2)

    R = D * cap
    xall[col] = ans[...]
    c_col = lambda s, to: rcopy(xall.at[s], xall.at[s], s_col.at[s, 0 if to is None else 1 + to], r_col.at[s],
                                c=sib if to is None else ypeers[to])
    started = [c_col(col, None)] + [c_col(col, k) for k in range(len(ypeers))]
    for c in started[1:]:
        c.start()
    started[0].start()
    slots = lambda ref, j: ref.at[pl.ds(pl.multiple_of(j * cap, 8), cap), :]
    c_ans = lambda j: rcopy(slots(ans, j), slots(ret, me), s_ans.at[j], r_ans.at[me], row=j)
    w_ans = lambda j: rcopy(slots(ans, j), slots(ret, j), s_ans.at[j], r_ans.at[j], row=j)
    sends(c_ans)
    here = pl.ds(pl.multiple_of(me * cap, 8), cap)
    ret[here, :] = ans[here, :]

    mine = xall[col]

    def block(s):
        part[pl.ds(pl.multiple_of(s * W, W), W), :] = lax.dot_general(
            mine, xall[s], TN, precision=HI, preferred_element_type=f32)
    block(col)
    for k in (0, 2, 1) if len(ypeers) == 3 else range(len(ypeers)):
        s = ypeers[k]
        c_col(s, None).wait_recv()
        f = c_col(s, None)
        f.start()
        started.append(f)
        block(s)
    for k in range(C // 2):
        s = lax.rem(sib + 2 * k, C)
        c_col(s, None).wait_recv()
        block(s)

    q = C * W // X
    xs = lambda j: part.at[pl.ds(pl.multiple_of(j * q, q), q), :]
    c_x = lambda j: rcopy(xs(j), xr.at[mx], s_x.at[j], r_x.at[mx], row=j * Z + mz)
    w_x = lambda j: rcopy(xs(j), xr.at[j], s_x.at[j], r_x.at[j], row=j * Z + mz)
    xpeers = [lax.rem(mx + k, X) for k in range(1, X)]
    for j in xpeers:
        c_x(j).start()
    xr[mx] = part[pl.ds(pl.multiple_of(mx * q, q), q), :]

    waits(w_ans, True)

    def keep(t, _):
        k, base = t // 16, t % 16
        for e in range(8):
            i = jnp.clip(owns[k, 0, base * 8 + e], 0, R - 1)
            sk_ref[pl.ds(t * 8 + e, 1), :] = ret[pl.ds(i, 1), :]
        return 0
    lax.fori_loop(0, S // 8, keep, 0)

    for j in xpeers:
        w_x(j).wait_recv()
    acc = xr[0]
    for j in range(1, X):
        acc = acc + xr[j]
    e = q // Z
    zs[...] = acc.reshape(Z, e, W)
    zpeers = lambda k: lax.rem(mz + k, Z)
    c_z = lambda j: rcopy(zs.at[j], zr.at[mz], s_z.at[j], r_z.at[mz], row=mx * Z + j)
    w_z = lambda j: rcopy(zs.at[j], zr.at[j], s_z.at[j], r_z.at[j], row=mx * Z + j)
    for k in range(1, Z):
        c_z(zpeers(k)).start()
    zr[mz] = zs[mz]
    for k in range(1, Z):
        w_z(zpeers(k)).wait_recv()
    acc = zr[0]
    for j in range(1, Z):
        acc = acc + zr[j]
    xg[mx, pl.ds(pl.multiple_of(mz * e, e), e), :] = acc / samples
    ze = lambda x, j: xg.at[x, pl.ds(pl.multiple_of(j * e, e), e), :]
    c_zg = lambda j: rcopy(ze(mx, mz), ze(mx, mz), s_zg.at[j], r_zg.at[mz], row=mx * Z + j)
    w_zg = lambda j: rcopy(ze(mx, j), ze(mx, j), s_zg.at[j], r_zg.at[j], row=mx * Z + j)
    for k in range(1, Z):
        c_zg(zpeers(k)).start()
    for k in range(1, Z):
        w_zg(zpeers(k)).wait_recv()
    c_xg = lambda j: rcopy(xg.at[mx], xg.at[mx], s_xg.at[j], r_xg.at[mx], row=j * Z + mz)
    w_xg = lambda j: rcopy(xg.at[j], xg.at[j], s_xg.at[j], r_xg.at[j], row=j * Z + mz)
    for j in xpeers:
        c_xg(j).start()
    for j in xpeers:
        w_xg(j).wait_recv()
    gram_ref[col] = xg[...].reshape(C * W, W)
    c_cg = lambda s, to: rcopy(gram_ref.at[s], gram_ref.at[s], s_cg.at[s, 0 if to is None else 1 + to], r_cg.at[s],
                               c=sib if to is None else ypeers[to])
    out = [c_cg(col, None)] + [c_cg(col, k) for k in range(len(ypeers))]
    for c in out[1:]:
        c.start()
    out[0].start()
    for k in (0, 2, 1) if len(ypeers) == 3 else range(len(ypeers)):
        s = ypeers[k]
        c_cg(s, None).wait_recv()
        f = c_cg(s, None)
        f.start()
        out.append(f)
    for k in range(C // 2):
        c_cg(lax.rem(sib + 2 * k, C), None).wait_recv()

    waits(w_req, False)
    waits(w_sec, False)
    waits(w_ans, False)
    for c in started + out:
        c.wait_send()
    for j in xpeers:
        w_x(j).wait_send()
        w_xg(j).wait_send()
    for k in range(1, Z):
        w_z(zpeers(k)).wait_send()
        w_zg(zpeers(k)).wait_send()


def exchange(a, signs, blocks, offs, X, Z, C):
    rows, W = a.shape
    D = X * Z
    S = offs.shape[0]
    cap = max(2, 2 * S // D)
    rb = rows // D
    R = D * cap
    q = C * W // X
    V = pltpu.VMEM
    dma = pltpu.SemaphoreType.DMA
    return pl.pallas_call(
        functools.partial(exchange_kernel, X, Z, C, 1.0 / math.sqrt(D * rows), float(D * S)),
        out_shape=(jax.ShapeDtypeStruct((C, C * W, W), f32), jax.ShapeDtypeStruct((S, W), f32)),
        in_specs=[pl.BlockSpec(memory_space=V)] * 4,
        out_specs=(pl.BlockSpec(memory_space=V), pl.BlockSpec(memory_space=V)),
        scratch_shapes=[
            V((rows, W), f32), V((rows, W), f32), V((rows + 8, W), f32),
            V((D, 1, 128), jnp.int32), V((D, 1, 128), jnp.int32), pltpu.SMEM((D, 1, 128), jnp.int32),
            V((S // 128, 1, 128), jnp.int32), pltpu.SMEM((S // 128, 1, 128), jnp.int32),
            V((R, W), f32), V((R, W), f32), V((C, R, W), f32),
            V((C * W, W), f32), V((X, q, W), f32), V((Z, q // Z, W), f32), V((Z, q // Z, W), f32), V((X, q, W), f32),
            dma((D,)), dma((D,)), dma((D,)), dma((D,)), dma((D,)), dma((D,)),
            dma((C, 1 + C // 2)), dma((C,)), dma((X,)), dma((X,)), dma((Z,)), dma((Z,)),
            dma((Z,)), dma((Z,)), dma((X,)), dma((X,)), dma((C, 1 + C // 2)), dma((C,)), dma((2,)),
        ],
        compiler_params=pltpu.CompilerParams(collective_id=0, has_side_effects=True, vmem_limit_bytes=48 * 2**20),
        name="exchange",
    )(a, signs.reshape(rows // 128, 128), blocks, offs.reshape(S // 128, 128))


PAN = 128
BLK = 16


def panel_factor(aug, upan):
    cur = aug[0:BLK, :]
    nblk = PAN // BLK
    for t in range(nblk):
        lo = t * BLK
        last = t == nblk - 1
        x = cur[:, lo:lo + BLK]
        C = [jnp.broadcast_to(x[:, k:k + 1], (BLK, PAN)) for k in range(BLK)]
        R = [cur[:, 0:PAN], cur[:, PAN:2 * PAN]]
        if not last:
            xt = jnp.transpose(cur[:, 0:PAN])[lo + BLK:lo + 2 * BLK, :]
            N = [jnp.broadcast_to(xt[:, k:k + 1], (BLK, PAN)) for k in range(BLK)]
            nxt = aug[lo + BLK:lo + 2 * BLK, :]
            if t > 0:
                done = upan[0:lo, :]
                nxt = nxt - lax.dot_general(done[:, lo + BLK:lo + 2 * BLK], done, TN,
                                            precision=lax.Precision.HIGHEST, preferred_element_type=f32)
            Rn = [nxt[:, 0:PAN], nxt[:, PAN:2 * PAN]]
        for k in range(BLK):
            rs = lax.rsqrt(C[k][k:k + 1, :])
            u = [R[h][k:k + 1, :] * rs for h in range(2)]
            for h in range(2):
                upan[lo + k:lo + k + 1, h * PAN:(h + 1) * PAN] = u[h]
            L = C[k] * rs
            if not last:
                Nl = N[k] * rs
            for c in range(k + 1, BLK):
                m = L[c:c + 1, :]
                if c < 8:
                    C[c] = C[c] - L * m
                else:
                    C[c] = C[c] - L * m
                if not last:
                    N[c] = N[c] - Nl * m
            for h in range(2):
                if k < BLK - 1:
                    R[h] = R[h] - L * u[h]
                if not last:
                    Rn[h] = Rn[h] - Nl * u[h]
        if not last:
            cur = jnp.concatenate(Rn, axis=1)


def chol_kernel(n, col_name, g_ref, out_ref, s, u, aug, upan):
    np_ = n // PAN
    for i in range(np_):
        for j in range(np_):
            s[i * PAN:(i + 1) * PAN, j * PAN:(j + 1) * PAN] = g_ref[i, j * PAN:(j + 1) * PAN, :]
    u[...] = jnp.zeros_like(u)
    ri = lax.broadcasted_iota(jnp.int32, (PAN, PAN), 0)
    ci = lax.broadcasted_iota(jnp.int32, (PAN, PAN), 1)

    def body(p, _):
        base = pl.multiple_of(p * PAN, PAN)
        aug[:, 0:PAN] = s[pl.ds(base, PAN), pl.ds(base, PAN)]
        aug[:, PAN:] = jnp.where(ri == ci, 1.0, 0.0).astype(f32)
        panel_factor(aug, upan)
        u[pl.ds(base, PAN), pl.ds(base, PAN)] = jnp.where(ri <= ci, upan[:, 0:PAN], 0.0)
        for pp in range(np_ - 1):
            @pl.when(p == pp)
            def _():
                a0, a1, rest = pp * PAN, (pp + 1) * PAN, n
                linv = jnp.where(ri >= ci, upan[:, PAN:], 0.0)
                w = lax.dot_general(linv, s[a0:a1, a1:], (((1,), (0,)), ((), ())),
                                    precision=lax.Precision.HIGHEST, preferred_element_type=f32)
                u[a0:a1, a1:] = w
                for q in range(pp + 1, np_):
                    q0 = q * PAN
                    s[q0:q0 + PAN, q0:] = s[q0:q0 + PAN, q0:] - lax.dot_general(
                        w[:, q0 - a1:q0 - a1 + PAN], w[:, q0 - a1:], TN,
                        precision=lax.Precision.HIGHEST, preferred_element_type=f32)
        return 0

    lax.fori_loop(0, np_, body, 0)
    mine = pl.multiple_of(lax.axis_index(col_name) * PAN, PAN)
    for j in range(np_):
        out_ref[j * PAN:(j + 1) * PAN, :] = jnp.transpose(u[pl.ds(mine, PAN), j * PAN:(j + 1) * PAN])


def chol(g):
    n = g.shape[1]
    return pl.pallas_call(
        functools.partial(chol_kernel, n, "col"),
        out_shape=jax.ShapeDtypeStruct((n, PAN), f32),
        in_specs=[pl.BlockSpec(memory_space=pltpu.VMEM)],
        out_specs=pl.BlockSpec(memory_space=pltpu.VMEM),
        scratch_shapes=[pltpu.VMEM((n, n), f32), pltpu.VMEM((n, n), f32),
                        pltpu.VMEM((PAN, 2 * PAN), f32), pltpu.VMEM((PAN, 2 * PAN), f32)],
        compiler_params=pltpu.CompilerParams(vmem_limit_bytes=48 * 2**20),
        name="chol",
    )(g)


def solution(mesh):
    x_size, z_size, c_size = 4, mesh.shape["row"] // 4, mesh.shape["col"]

    def shards(matrix, row_signs, sample_block, sample_offset):
        gram, sketch = exchange(matrix, row_signs, sample_block, sample_offset, x_size, z_size, c_size)
        return sketch, chol(gram)

    placed = (P("row", "col"), P("row"), P("row", None), P("row"))
    return jax.shard_map(
        shards,
        mesh=mesh,
        in_specs=placed,
        out_specs=(P("row", "col"), P(None, "col")),
        check_vma=False,
    )
```

time: 428 us -> 190 us (0.44); the launches traced: 420 us -> 190 us
  waiting for transfers between devices: 211 us -> 0 us
  Pallas kernels: 34.1 us -> 185 us
  blocking collectives: 90.9 us -> 0 us
  starting transfers between devices: 27.4 us -> 0 us
  local copies, waits for them, and re-layouts: 27.6 us -> 4.06 us
  between operations: 14.2 us -> 0.66 us
  matrix products: 8.92 us -> 0 us
  other arithmetic: 6.04 us -> 0 us
    all_gather x2 -> x0, waiting for transfers between devices: 156 us -> none  [the longest x1 129 us: shards(): lax.all_gather(lax.all_gather(summed, 'col', axis=1, tiled=True), 'row',...]
    pallas_call x1 -> x2, Pallas kernels: 34.1 us -> 185 us  [the longest x1 152 us: exchange(): pl.pallas_call(functools.partial(exchange_kernel, X, Z, C, 1.0 / math.sqr...]
    all_to_all x2 -> x0, blocking collectives: 74.3 us -> none  [the longest x1 45.1 us: shards(): lax.all_to_all(pieces, 'row', split_axis=0, concat_axis=0, tiled=True)]
    all_to_all x2 -> x0, waiting for transfers between devices: 54.7 us -> none  [the longest x1 48.1 us: shards(): lax.all_to_all(sectioned, 'row', split_axis=0, concat_axis=0, tiled=True)]
    all_to_all x2 -> x0, starting transfers between devices: 27.1 us -> none  [the longest x1 19.1 us: shards(): lax.all_to_all(outgoing, 'row', split_axis=0, concat_axis=0, tiled=True)]
    scatter x1 -> x0, local copies, waits for them, and re-layouts: 21.2 us -> none  [shards(): jnp.zeros((devices, capacity), jnp.int32).at[blocks, slots]]
    all_gather x1 -> x0, blocking collectives: 16.6 us -> none  [shards(): lax.all_gather(summed, 'col', axis=1, tiled=True)]
    dot_general x4 -> x0, matrix products: 8.92 us -> none  [the longest x1 3.03 us: shards(): jnp.dot(panel.T, sketch, precision=highest, preferred_element_type=jnp.fl...]
  transfers between devices with their start and end apart: 4 -> 0, of which waited for: 4 -> 0; matrix products, arithmetic and copies ran while one was open for 2% -> 0% of each run, Pallas kernels for 0% -> 0%
where the time goes in v2:
time: 190 us
  Pallas kernels  185 us (97%)
  local copies, waits for them, and re-layouts  4.06 us (2%)
    pallas_call x1, Pallas kernels, exchange(): pl.pallas_call(functools.partial(exchange_kernel, X, Z, C, 1.0 / math.sqr...  152 us
    pallas_call x1, Pallas kernels, chol(): pl.pallas_call(functools.partial(chol_kernel, n, 'col'), out_shape=jax.Sh...  33 us
    unnamed x8, local copies, waits for them, and re-layouts  4.06 us

profile of v2, /device:TPU:1, one launch (start us, length us, event | category | flops | bytes accessed | tf_op | source)
XLA Modules:
  0.0 189.8 jit_solution(6315391137905382154)
XLA Ops:
  0.6 0.8 copy.6.blk_ref
  1.4 0.0 copy-start
  1.5 1.2 copy-done
  2.7 0.0 copy-start.1
  2.7 0.7 copy-done.1
  3.4 0.0 copy-start.2
  3.4 0.7 copy-done.2
  4.1 152.1 %exchange.1 = (f32[8,1024,128]{2,1,0:T(8,128)S(1)}, f32[256,128]{1,0:T(8,128)S(1)}) custom-call(f32[2048,128]{1,0:T(8,128)S(1)} %copy-done, s32[16,128]{1,0:T(8,128)S(1)} %bitcast.2, s32[256,1]{1,0:T(8,128)S(1)} %copy.6.blk_ref, s32[2,128]{1,0:T(2,128)S(1)} %bitcast.3), custom_call_target="tpu_custom_call" | custom-call | tf_op jit(solution)/shard_map/exchange/pallas_call | solution.py:288
  156.2 33.0 %chol.1 = f32[1024,128]{1,0:T(8,128)} custom-call(f32[8,1024,128]{2,1,0:T(8,128)S(1)} %get-tuple-element.5.g_ref), custom_call_target="tpu_custom_call" | custom-call | tf_op jit(solution)/shard_map/chol/pallas_call | solution.py:393
  189.2 0.7 copy.8
Async XLA Ops:
  1.4 1.2 copy-start
  2.7 0.7 copy-start.1
  3.4 0.7 copy-start.2

commit v3 on v2

v3 whole, which is shorter than its diff:
```python
import functools
import math

import jax
import jax.numpy as jnp
from jax import lax
from jax.experimental import pallas as pl
from jax.experimental.pallas import tpu as pltpu
from jax.sharding import PartitionSpec as P

f32, bf16 = jnp.float32, jnp.bfloat16
TN = (((0,), (0,)), ((), ()))
HI = lax.Precision.HIGHEST


def butterflies(v):
    n, step = len(v), 1
    while step < n:
        v = [v[i] + v[i + step] if not i & step else v[i - step] - v[i] for i in range(n)]
        step *= 2
    return v


def mix_pass(src, dst, rows, low, bits, scale=None):
    n, stride = 1 << bits, 1 << low
    tiles = stride // 8
    groups = rows // (n * stride)

    def body(t, _):
        g, j = t // tiles, t % tiles
        base = g * (n * stride) + j * 8
        v = [src[pl.ds(pl.multiple_of(base + i * stride, 8), 8), :] for i in range(n)]
        v = butterflies(v)
        for i in range(n):
            dst[pl.ds(pl.multiple_of(base + i * stride, 8), 8), :] = v[i] if scale is None else v[i] * scale
        return 0

    lax.fori_loop(0, groups * tiles, body, 0, unroll=2 if groups * tiles % 2 == 0 else 1)


PAN = 128
BLK = 16


def panel_factor(aug, upan):
    cur = aug[0:BLK, :]
    nblk = PAN // BLK
    for t in range(nblk):
        lo = t * BLK
        last = t == nblk - 1
        x = cur[:, lo:lo + BLK]
        C = [jnp.broadcast_to(x[:, k:k + 1], (BLK, PAN)) for k in range(BLK)]
        R = [cur[:, 0:PAN], cur[:, PAN:2 * PAN]]
        if not last:
            xt = jnp.transpose(cur[:, 0:PAN])[lo + BLK:lo + 2 * BLK, :]
            N = [jnp.broadcast_to(xt[:, k:k + 1], (BLK, PAN)) for k in range(BLK)]
            nxt = aug[lo + BLK:lo + 2 * BLK, :]
            if t > 0:
                done = upan[0:lo, :]
                nxt = nxt - lax.dot_general(done[:, lo + BLK:lo + 2 * BLK], done, TN,
                                            precision=lax.Precision.HIGHEST, preferred_element_type=f32)
            Rn = [nxt[:, 0:PAN], nxt[:, PAN:2 * PAN]]
        for k in range(BLK):
            rs = lax.rsqrt(C[k][k:k + 1, :])
            u = [R[h][k:k + 1, :] * rs for h in range(2)]
            for h in range(2):
                upan[lo + k:lo + k + 1, h * PAN:(h + 1) * PAN] = u[h]
            L = C[k] * rs
            if not last:
                Nl = N[k] * rs
            for c in range(k + 1, BLK):
                m = L[c:c + 1, :]
                if c < 8:
                    C[c] = C[c] - L * m
                else:
                    C[c] = C[c] - L * m
                if not last:
                    N[c] = N[c] - Nl * m
            for h in range(2):
                if k < BLK - 1:
                    R[h] = R[h] - L * u[h]
                if not last:
                    Rn[h] = Rn[h] - Nl * u[h]
        if not last:
            cur = jnp.concatenate(Rn, axis=1)


def exchange_kernel(X, Z, C, norm, samples,
                    a_ref, sign_ref, blk_ref, off_ref,
                    fac_ref, sk_ref,
                    v, recv, table, req, reqr, reqs, own, owns, ans, ret, xall, part, xr, zs, zr, gb, u, aug, upan,
                    s_req, r_req, s_sec, r_sec, s_ans, r_ans, s_col, r_col, s_x, r_x, s_z, r_z,
                    s_zg, r_zg, s_xg, r_xg, s_cg, s_fw, r_cg, l_sem):
    D = X * Z
    rows = a_ref.shape[0]
    rb = rows // D
    W = a_ref.shape[1]
    cap = ans.shape[0] // D
    S = blk_ref.shape[0]
    me, col = lax.axis_index("row"), lax.axis_index("col")
    mx, mz = me // Z, me % Z
    sib = col + 1 - 2 * (col % 2)

    def rcopy(src, dst, ss, rs, row=None, c=None):
        dev = {"row": row} if c is None else {"col": c}
        return pltpu.make_async_remote_copy(src_ref=src, dst_ref=dst, send_sem=ss, recv_sem=rs,
                                            device_id=dev, device_id_type=pl.DeviceIdType.MESH)

    bar = pltpu.get_barrier_semaphore()

    def greet(k, _):
        pl.semaphore_signal(bar, inc=1, device_id={"row": lax.rem(me + k, D)}, device_id_type=pl.DeviceIdType.MESH)
        return 0
    lax.fori_loop(1, D, greet, 0)
    ypeers = [lax.rem(col + 2 * k, C) for k in range(1, C // 2)]
    for c in [sib] + ypeers:
        pl.semaphore_signal(bar, inc=1, device_id={"col": c}, device_id_type=pl.DeviceIdType.MESH)

    blocks = blk_ref[...]
    lane = lax.broadcasted_iota(jnp.int32, (S, 128), 1)
    onehot = (blocks == lane).astype(f32)
    ri = lax.broadcasted_iota(jnp.int32, (S, S), 0)
    ci = lax.broadcasted_iota(jnp.int32, (S, S), 1)
    before = jnp.dot((ci < ri).astype(bf16), onehot.astype(bf16), preferred_element_type=f32)
    slot = jnp.sum(before * onehot, axis=1, keepdims=True)
    offs = jnp.transpose(jnp.concatenate(
        [off_ref[...].astype(f32), jnp.zeros((128 - S // 128, 128), f32)], axis=0))
    offc = jnp.concatenate([offs[:, k:k + 1] for k in range(S // 128)], axis=0)
    val = jnp.where(lane.astype(f32) == slot, offc - float(rows), 0.0)
    wanted = lax.dot_general(onehot, val, TN, precision=HI, preferred_element_type=f32) + float(rows)
    wanted = wanted.astype(jnp.int32)
    for j in range(D):
        req[j] = wanted[j:j + 1, :]
    place = (blocks.astype(f32) * float(cap) + slot)
    for k in range(S // 128):
        t = jnp.transpose(jnp.broadcast_to(place[k * 128:(k + 1) * 128, :], (128, 128)))
        own[k] = t[0:1, :].astype(jnp.int32)
    oc = pltpu.make_async_copy(own, owns, l_sem.at[0])
    oc.start()

    nb = rows // 128
    st = jnp.transpose(jnp.concatenate([sign_ref[...].astype(f32), jnp.zeros((128 - nb, 128), f32)], axis=0))
    for j in range(nb):
        v[j * 128:(j + 1) * 128, :] = a_ref[j * 128:(j + 1) * 128, :] * jnp.broadcast_to(st[:, j:j + 1], (128, W))

    def low_bits(g, _):
        base = pl.multiple_of(g * 64, 64)
        w = butterflies([v[pl.ds(base + k, 8, stride=8), :] for k in range(8)])
        for k in range(8):
            v[pl.ds(base + k, 8, stride=8), :] = w[k]
        return 0
    lax.fori_loop(0, rows // 64, low_bits, 0, unroll=2)
    left, low = rows.bit_length() - 1 - 3, 3
    while left:
        b = min(3, left)
        mix_pass(v, v, rows, low, b)
        low, left = low + b, left - b

    pl.semaphore_wait(bar, D - 1 + 1 + len(ypeers))

    def peer_of(k):
        return lax.rem(me + jnp.where(k % 2 == 1, (k + 1) // 2, D - k // 2), D)

    def sends(fn):
        def go(k, _):
            fn(peer_of(k)).start()
            return 0
        lax.fori_loop(1, D, go, 0)

    def waits(fn, recv_side):
        def go(k, _):
            c = fn(lax.rem(me + k, D))
            if recv_side:
                c.wait_recv()
            else:
                c.wait_send()
            return 0
        lax.fori_loop(1, D, go, 0)

    c_req = lambda j: rcopy(req.at[j], reqr.at[me], s_req.at[j], r_req.at[me], row=j)
    w_req = lambda j: rcopy(req.at[j], reqr.at[j], s_req.at[j], r_req.at[j], row=j)
    sec = lambda j: v.at[pl.ds(pl.multiple_of(j * rb, rb), rb), :]
    got = lambda j: recv.at[pl.ds(pl.multiple_of(j * rb, rb), rb), :]
    c_sec = lambda j: rcopy(sec(j), got(me), s_sec.at[j], r_sec.at[me], row=j)
    w_sec = lambda j: rcopy(sec(j), got(j), s_sec.at[j], r_sec.at[j], row=j)
    sends(c_req)
    sends(c_sec)
    reqr[me] = req[me]
    recv[pl.ds(pl.multiple_of(me * rb, rb), rb), :] = v[pl.ds(pl.multiple_of(me * rb, rb), rb), :]
    table[rows:rows + 8, :] = jnp.zeros((8, W), f32)
    waits(w_req, True)
    rc = pltpu.make_async_copy(reqr, reqs, l_sem.at[1])
    rc.start()
    rc.wait()
    oc.wait()
    waits(w_sec, True)

    lowb = rb.bit_length() - 1
    left, low, first = D.bit_length() - 1, lowb, True
    while left:
        b = min(3, left)
        left -= b
        mix_pass(recv if first else table, table, rows, low, b, norm if left == 0 else None)
        low, first = low + b, False

    def answer(j, _):
        for c in range(cap):
            ans[pl.ds(j * cap + c, 1), :] = table[pl.ds(jnp.clip(reqs[j, 0, c], 0, rows), 1), :]
        return 0
    lax.fori_loop(0, D, answer, 0, unroll=2)

    R = D * cap
    xall[col] = ans[...]
    c_col = lambda s, to: rcopy(xall.at[s], xall.at[s], s_col.at[s, 0 if to is None else 1 + to], r_col.at[s],
                                c=sib if to is None else ypeers[to])
    started = [c_col(col, None)] + [c_col(col, k) for k in range(len(ypeers))]
    for c in started[1:]:
        c.start()
    started[0].start()
    slots = lambda ref, j: ref.at[pl.ds(pl.multiple_of(j * cap, 8), cap), :]
    c_ans = lambda j: rcopy(slots(ans, j), slots(ret, me), s_ans.at[j], r_ans.at[me], row=j)
    w_ans = lambda j: rcopy(slots(ans, j), slots(ret, j), s_ans.at[j], r_ans.at[j], row=j)
    sends(c_ans)
    here = pl.ds(pl.multiple_of(me * cap, 8), cap)
    ret[here, :] = ans[here, :]

    mine = jnp.transpose(xall[col])

    def block(s):
        part[pl.ds(pl.multiple_of(s * W, W), W), :] = jnp.transpose(
            jnp.dot(mine, xall[s], precision=HI, preferred_element_type=f32))
    block(col)
    for k in (0, 2, 1) if len(ypeers) == 3 else range(len(ypeers)):
        s = ypeers[k]
        c_col(s, None).wait_recv()
        f = c_col(s, None)
        f.start()
        started.append(f)
        block(s)
    for k in range(C // 2):
        s = lax.rem(sib + 2 * k, C)
        c_col(s, None).wait_recv()
        block(s)

    q = C * W // X
    xs = lambda j: part.at[pl.ds(pl.multiple_of(j * q, q), q), :]
    c_x = lambda j: rcopy(xs(j), xr.at[mx], s_x.at[j], r_x.at[mx], row=j * Z + mz)
    w_x = lambda j: rcopy(xs(j), xr.at[j], s_x.at[j], r_x.at[j], row=j * Z + mz)
    xpeers = [lax.rem(mx + k, X) for k in range(1, X)]
    for j in xpeers:
        c_x(j).start()
    xr[mx] = part[pl.ds(pl.multiple_of(mx * q, q), q), :]

    waits(w_ans, True)

    def keep(t, _):
        k, base = t // 16, t % 16
        for e in range(8):
            i = jnp.clip(owns[k, 0, base * 8 + e], 0, R - 1)
            sk_ref[pl.ds(t * 8 + e, 1), :] = ret[pl.ds(i, 1), :]
        return 0
    lax.fori_loop(0, S // 8, keep, 0)

    for j in xpeers:
        w_x(j).wait_recv()
    acc = xr[0]
    for j in range(1, X):
        acc = acc + xr[j]
    e = q // Z
    zs[...] = acc.reshape(Z, e, W)
    zpeers = lambda k: lax.rem(mz + k, Z)
    c_z = lambda j: rcopy(zs.at[j], zr.at[mz], s_z.at[j], r_z.at[mz], row=mx * Z + j)
    w_z = lambda j: rcopy(zs.at[j], zr.at[j], s_z.at[j], r_z.at[j], row=mx * Z + j)
    for k in range(1, Z):
        c_z(zpeers(k)).start()
    zr[mz] = zs[mz]
    for k in range(1, Z):
        w_z(zpeers(k)).wait_recv()
    acc = zr[0]
    for j in range(1, Z):
        acc = acc + zr[j]
    gb[col, pl.ds(pl.multiple_of(mx * q + mz * e, e), e), :] = acc / samples
    ze = lambda j: gb.at[col, pl.ds(pl.multiple_of(mx * q + j * e, e), e), :]
    c_zg = lambda j: rcopy(ze(mz), ze(mz), s_zg.at[j], r_zg.at[mz], row=mx * Z + j)
    w_zg = lambda j: rcopy(ze(j), ze(j), s_zg.at[j], r_zg.at[j], row=mx * Z + j)
    for k in range(1, Z):
        c_zg(zpeers(k)).start()
    for k in range(1, Z):
        w_zg(zpeers(k)).wait_recv()
    per = C // X
    gblk = lambda s, p: gb.at[s, pl.ds(pl.multiple_of(p * W, W), W), :]
    c_xg = lambda p, j: rcopy(gblk(col, p), gblk(col, p), s_xg.at[p, j], r_xg.at[p], row=j * Z + mz)
    c_cg = lambda p, k: rcopy(gblk(col, p), gblk(col, p), s_cg.at[p, k], r_cg.at[col, p], c=ypeers[k])
    c_fw = lambda s, p: rcopy(gblk(s, p), gblk(s, p), s_fw.at[s, p], r_cg.at[s, p], c=sib)

    def along_x(p):
        @pl.when((mx == p // per) & (p <= col))
        def _():
            for j in xpeers:
                c_xg(p, j).start()

    def over_col(p):
        @pl.when(p <= col)
        def _():
            @pl.when(mx != p // per)
            def _():
                c_xg(p, mx).wait_recv()
            for k in (1, 0, 2) if len(ypeers) == 3 else range(len(ypeers)):
                c_cg(p, k).start()
            c_fw(col, p).start()

    def pass_on(p):
        for s in ypeers:
            @pl.when(p <= s)
            def _():
                c_fw(s, p).wait_recv()
                c_fw(s, p).start()

    def arrived(p):
        for k in range(C // 2):
            s = lax.rem(sib + 2 * k, C)

            @pl.when(p <= s)
            def _():
                c_fw(s, p).wait_recv()

    def each(fn, lo, hi):
        lax.fori_loop(lo, hi, lambda p, _: (fn(p), 0)[1], 0)
    each(along_x, 0, C)
    each(over_col, 0, 2)
    pass_on(0)

    u[...] = jnp.zeros_like(u)
    pr = lax.broadcasted_iota(jnp.int32, (W, W), 0)
    pc = lax.broadcasted_iota(jnp.int32, (W, W), 1)

    def panel(p, _):
        @pl.when(p + 2 < C)
        def _():
            over_col(p + 2)

        @pl.when(p + 1 < C)
        def _():
            pass_on(p + 1)
        arrived(p)
        base = pl.multiple_of(p * W, W)
        for pp in range(C):
            @pl.when(p == pp)
            def _():
                a0 = pp * W
                for t in range(pp, C):
                    u[a0:a0 + W, t * W:(t + 1) * W] = gb[t, a0:a0 + W, :]
                if pp:
                    u[a0:a0 + W, a0:] = u[a0:a0 + W, a0:] - lax.dot_general(
                        u[0:a0, a0:a0 + W], u[0:a0, a0:], TN, precision=HI, preferred_element_type=f32)
        aug[:, 0:W] = u[pl.ds(base, W), pl.ds(base, W)]
        aug[:, W:] = jnp.where(pr == pc, 1.0, 0.0).astype(f32)
        panel_factor(aug, upan)
        u[pl.ds(base, W), pl.ds(base, W)] = jnp.where(pr <= pc, upan[:, 0:W], 0.0)
        for pp in range(C - 1):
            @pl.when(p == pp)
            def _():
                a0, a1 = pp * W, (pp + 1) * W
                linv = jnp.where(pr >= pc, upan[:, W:], 0.0)
                u[a0:a1, a1:] = jnp.dot(linv, u[a0:a1, a1:], precision=HI, preferred_element_type=f32)
        return 0

    lax.fori_loop(0, C, panel, 0)
    here = pl.ds(pl.multiple_of(col * W, W), W)
    for j in range(C):
        fac_ref[j * W:(j + 1) * W, :] = jnp.transpose(u[here, j * W:(j + 1) * W])

    waits(w_req, False)
    waits(w_sec, False)
    waits(w_ans, False)
    for c in started:
        c.wait_send()
    for j in xpeers:
        w_x(j).wait_send()

    def left(p):
        @pl.when(p <= col)
        def _():
            @pl.when(mx == p // per)
            def _():
                for j in xpeers:
                    c_xg(p, j).wait_send()
            for k in range(len(ypeers)):
                c_cg(p, k).wait_send()
            c_fw(col, p).wait_send()
        for s in ypeers:
            @pl.when(p <= s)
            def _():
                c_fw(s, p).wait_send()
    each(left, 0, C)
    for k in range(1, Z):
        w_z(zpeers(k)).wait_send()
        w_zg(zpeers(k)).wait_send()


def exchange(a, signs, blocks, offs, X, Z, C):
    rows, W = a.shape
    D = X * Z
    S = offs.shape[0]
    cap = max(2, 2 * S // D)
    rb = rows // D
    R = D * cap
    q = C * W // X
    V = pltpu.VMEM
    dma = pltpu.SemaphoreType.DMA
    return pl.pallas_call(
        functools.partial(exchange_kernel, X, Z, C, 1.0 / math.sqrt(D * rows), float(D * S)),
        out_shape=(jax.ShapeDtypeStruct((C * W, W), f32), jax.ShapeDtypeStruct((S, W), f32)),
        in_specs=[pl.BlockSpec(memory_space=V)] * 4,
        out_specs=(pl.BlockSpec(memory_space=V), pl.BlockSpec(memory_space=V)),
        scratch_shapes=[
            V((rows, W), f32), V((rows, W), f32), V((rows + 8, W), f32),
            V((D, 1, 128), jnp.int32), V((D, 1, 128), jnp.int32), pltpu.SMEM((D, 1, 128), jnp.int32),
            V((S // 128, 1, 128), jnp.int32), pltpu.SMEM((S // 128, 1, 128), jnp.int32),
            V((R, W), f32), V((R, W), f32), V((C, R, W), f32),
            V((C * W, W), f32), V((X, q, W), f32), V((Z, q // Z, W), f32), V((Z, q // Z, W), f32),
            V((C, C * W, W), f32), V((C * W, C * W), f32), V((W, 2 * W), f32), V((W, 2 * W), f32),
            dma((D,)), dma((D,)), dma((D,)), dma((D,)), dma((D,)), dma((D,)),
            dma((C, 1 + C // 2)), dma((C,)), dma((X,)), dma((X,)), dma((Z,)), dma((Z,)),
            dma((Z,)), dma((Z,)), dma((C, X)), dma((C,)), dma((C, C // 2)), dma((C, C)), dma((C, C)), dma((2,)),
        ],
        compiler_params=pltpu.CompilerParams(collective_id=0, has_side_effects=True, vmem_limit_bytes=48 * 2**20),
        name="exchange",
    )(a, signs.reshape(rows // 128, 128), blocks, offs.reshape(S // 128, 128))


def solution(mesh):
    x_size, z_size, c_size = 4, mesh.shape["row"] // 4, mesh.shape["col"]

    def shards(matrix, row_signs, sample_block, sample_offset):
        factor, sketch = exchange(matrix, row_signs, sample_block, sample_offset, x_size, z_size, c_size)
        return sketch, factor

    placed = (P("row", "col"), P("row"), P("row", None), P("row"))
    return jax.shard_map(
        shards,
        mesh=mesh,
        in_specs=placed,
        out_specs=(P("row", "col"), P(None, "col")),
        check_vma=False,
    )
```

time: 190 us -> 169 us (0.89); the launches traced: 190 us -> 166 us
  Pallas kernels: 185 us -> 161 us
    pallas_call x1 -> x0, Pallas kernels: 33 us -> none  [chol(): pl.pallas_call(functools.partial(chol_kernel, n, 'col'), out_shape=jax.Sh...]
    pallas_call x1, Pallas kernels: 152 us -> 161 us  [exchange(): pl.pallas_call(functools.partial(exchange_kernel, X, Z, C, 1.0 / math.sqr...]
    unnamed x8 -> x11, local copies, waits for them, and re-layouts: 4.06 us -> 4.04 us
where the time goes in v3:
time: 169 us; the launch traced here: 166 us
  Pallas kernels  161 us (95%)
  local copies, waits for them, and re-layouts  4.04 us (2%)
    pallas_call x1, Pallas kernels, exchange(): pl.pallas_call(functools.partial(exchange_kernel, X, Z, C, 1.0 / math.sqr...  161 us
    unnamed x11, local copies, waits for them, and re-layouts  4.04 us

profile of v3, /device:TPU:1, one launch (start us, length us, event | category | flops | bytes accessed | tf_op | source)
XLA Modules:
  0.0 165.7 jit_solution(10042720304078387408)
XLA Ops:
  0.6 0.0 copy-start.3
  0.6 0.7 copy-done.3
  1.3 0.0 copy-start.1
  1.3 0.0 copy-start.2
  1.3 0.1 copy.6.blk_ref
  1.5 0.6 copy-done.1
  2.0 0.0 copy-done.2
  2.0 0.0 copy-start
  2.0 1.2 copy-done
  3.2 161.0 %exchange.1 = (f32[1024,128]{1,0:T(8,128)S(1)}, f32[256,128]{1,0:T(8,128)S(1)}) custom-call(f32[2048,128]{1,0:T(8,128)S(1)} %copy-done, s32[16,128]{1,0:T(8,128)S(1)} %bitcast.2, s32[256,1]{1,0:T(8,128)S(1)} %copy.6.blk_ref, s32[2,128]{1,0:T(2,128)S(1)} %bitcast.3), custom_call_target="tpu_custom_call" | custom-call | tf_op jit(solution)/shard_map/exchange/pallas_call | solution.py:411
  164.2 0.7 copy.9
  164.9 0.8 copy.10
Async XLA Ops:
  0.6 0.7 copy-start.3
  1.3 0.7 copy-start.1
  1.3 0.7 copy-start.2
  2.0 1.2 copy-start

commit v4 on v3

v4 whole, which is shorter than its diff:
```python
import functools
import math

import jax
import jax.numpy as jnp
from jax import lax
from jax.experimental import pallas as pl
from jax.experimental.pallas import tpu as pltpu
from jax.sharding import PartitionSpec as P

f32, bf16 = jnp.float32, jnp.bfloat16
TN = (((0,), (0,)), ((), ()))
HI = lax.Precision.HIGHEST


def butterflies(v):
    n, step = len(v), 1
    while step < n:
        v = [v[i] + v[i + step] if not i & step else v[i - step] - v[i] for i in range(n)]
        step *= 2
    return v


def mix_pass(src, dst, rows, low, bits, scale=None):
    n, stride = 1 << bits, 1 << low
    tiles = stride // 8
    groups = rows // (n * stride)

    def body(t, _):
        g, j = t // tiles, t % tiles
        base = g * (n * stride) + j * 8
        v = [src[pl.ds(pl.multiple_of(base + i * stride, 8), 8), :] for i in range(n)]
        v = butterflies(v)
        for i in range(n):
            dst[pl.ds(pl.multiple_of(base + i * stride, 8), 8), :] = v[i] if scale is None else v[i] * scale
        return 0

    lax.fori_loop(0, groups * tiles, body, 0, unroll=2 if groups * tiles % 2 == 0 else 1)


PAN = 128
BLK = 16


def panel_factor(aug, upan):
    wide = 2 * PAN
    lanes = wide // PAN
    cur = [[aug[8 * r:8 * r + 8, h * PAN:(h + 1) * PAN] for h in range(lanes)] for r in range(BLK // 8)]
    nblk, sub = PAN // BLK, BLK // 8
    for t in range(nblk):
        lo = t * BLK
        last = t == nblk - 1
        C = [[jnp.broadcast_to(cur[r][0][:, lo + k:lo + k + 1], (8, PAN)) for r in range(sub)] for k in range(BLK)]
        if not last:
            xt = jnp.transpose(jnp.concatenate([cur[r][0] for r in range(sub)], axis=0))[lo + BLK:lo + 2 * BLK, :]
            N = [[jnp.broadcast_to(xt[8 * r:8 * r + 8, k:k + 1], (8, PAN)) for r in range(sub)] for k in range(BLK)]
            nxt = aug[lo + BLK:lo + 2 * BLK, :]
            if t > 0:
                done = upan[0:lo, :]
                nxt = nxt - lax.dot_general(done[:, lo + BLK:lo + 2 * BLK], done, TN,
                                            precision=HI, preferred_element_type=f32)
            acc = [[None] * lanes for _ in range(sub)]
        R = cur
        for k in range(BLK):
            rs = lax.rsqrt(C[k][k // 8][k % 8:k % 8 + 1, :])
            u = [R[k // 8][h][k % 8:k % 8 + 1, :] * rs for h in range(lanes)]
            for h in range(lanes):
                upan[lo + k:lo + k + 1, h * PAN:(h + 1) * PAN] = u[h]
            first = (k + 1) // 8
            L = [C[k][r] * rs if r >= first else None for r in range(sub)]
            Nl = [N[k][r] * rs for r in range(sub)] if not last else None
            for c in range(k + 1, BLK):
                m = L[c // 8][c % 8:c % 8 + 1, :]
                for r in range(c // 8, sub):
                    C[c][r] = C[c][r] - L[r] * m
                if not last:
                    for r in range(sub):
                        N[c][r] = N[c][r] - Nl[r] * m
            for h in range(lanes):
                for r in range(first, sub):
                    R[r][h] = R[r][h] - L[r] * u[h]
                if not last:
                    for r in range(sub):
                        acc[r][h] = Nl[r] * u[h] if acc[r][h] is None else acc[r][h] + Nl[r] * u[h]
        if not last:
            cur = [[nxt[8 * r:8 * r + 8, h * PAN:(h + 1) * PAN] - acc[r][h] for h in range(lanes)] for r in range(sub)]


def exchange_kernel(X, Z, C, norm, samples,
                    a_ref, sign_ref, blk_ref, off_ref,
                    fac_ref, sk_ref,
                    v, sign, pos, recv, table, req, reqx, reqr, reqs, own, owns, ans, ansz, ret, xall, part, xr, zs, zr,
                    gb, u, aug, upan,
                    s_rx, r_rx, s_rz, r_rz, s_sec, r_sec, s_az, r_az, s_ax, r_ax, s_col, r_col, s_x, r_x, s_z, r_z,
                    s_zg, r_zg, s_xg, r_xg, s_cg, s_fw, s_rl, r_cg, l_sem):
    D = X * Z
    rows, W = v.shape
    rb = rows // D
    cap = ret.shape[0] // D
    SR = blk_ref.shape[0]
    S = SR * 128
    me, col = lax.axis_index("row"), lax.axis_index("col")
    mx, mz = me // Z, me % Z
    sib = col + 1 - 2 * (col % 2)

    def rcopy(src, dst, ss, rs, row=None, c=None):
        dev = {"row": row} if c is None else {"col": c}
        return pltpu.make_async_remote_copy(src_ref=src, dst_ref=dst, send_sem=ss, recv_sem=rs,
                                            device_id=dev, device_id_type=pl.DeviceIdType.MESH)

    bar = pltpu.get_barrier_semaphore()

    def greet(k, _):
        pl.semaphore_signal(bar, inc=1, device_id={"row": lax.rem(me + k, D)}, device_id_type=pl.DeviceIdType.MESH)
        return 0
    lax.fori_loop(1, D, greet, 0)
    ypeers = [lax.rem(col + 2 * k, C) for k in range(1, C // 2)]
    for c in [sib] + ypeers:
        pl.semaphore_signal(bar, inc=1, device_id={"col": c}, device_id_type=pl.DeviceIdType.MESH)

    fetch = [pltpu.make_async_copy(src, dst, l_sem.at[2 + k]) for k, (src, dst) in enumerate(
        [(blk_ref, pos.at[0]), (off_ref, pos.at[1]), (sign_ref, sign), (a_ref, v)])]
    for c in fetch:
        c.start()
    nb = rows // 128
    fetch[2].wait()
    fetch[3].wait()
    st = jnp.transpose(jnp.concatenate([sign[...].astype(f32), jnp.zeros((128 - nb, 128), f32)], axis=0))
    for j in range(nb):
        v[j * 128:(j + 1) * 128, :] = v[j * 128:(j + 1) * 128, :] * jnp.broadcast_to(st[:, j:j + 1], (128, W))

    def low_bits(g, _):
        base = pl.multiple_of(g * 64, 64)
        w = butterflies([v[pl.ds(base + k, 8, stride=8), :] for k in range(8)])
        for k in range(8):
            v[pl.ds(base + k, 8, stride=8), :] = w[k]
        return 0
    lax.fori_loop(0, rows // 64, low_bits, 0, unroll=2)
    left, low = rows.bit_length() - 1 - 3, 3
    while left:
        b = min(3, left)
        mix_pass(v, v, rows, low, b)
        low, left = low + b, left - b

    pl.semaphore_wait(bar, D - 1 + 1 + len(ypeers))

    def peer_of(k):
        return lax.rem(me + jnp.where(k % 2 == 1, (k + 1) // 2, D - k // 2), D)

    def sends(fn):
        def go(k, _):
            fn(peer_of(k)).start()
            return 0
        lax.fori_loop(1, D, go, 0)

    xpeers = [lax.rem(mx + k, X) for k in range(1, X)]
    zpeers = lambda k: lax.rem(mz + k, Z)
    c_rx = lambda j: rcopy(req.at[j], reqx.at[mx], s_rx.at[j], r_rx.at[mx], row=j * Z + mz)
    w_rx = lambda j: rcopy(req.at[j], reqx.at[j], s_rx.at[j], r_rx.at[j], row=j * Z + mz)
    c_rz = lambda j: rcopy(reqx.at[:, j], reqr.at[:, mz], s_rz.at[j], r_rz.at[mz], row=mx * Z + j)
    w_rz = lambda j: rcopy(reqx.at[:, j], reqr.at[:, j], s_rz.at[j], r_rz.at[j], row=mx * Z + j)
    sec = lambda j: v.at[pl.ds(pl.multiple_of(j * rb, rb), rb), :]
    got = lambda j: recv.at[pl.ds(pl.multiple_of(j * rb, rb), rb), :]
    c_sec = lambda j: rcopy(sec(j), got(me), s_sec.at[0], r_sec.at[0], row=j)
    others = pl.ds(0, (D - 1) * rb)
    all_sec = rcopy(v.at[others, :], recv.at[others, :], s_sec.at[0], r_sec.at[0], row=lax.rem(me + 1, D))
    sends(c_sec)
    fetch[0].wait()
    fetch[1].wait()

    both = jnp.transpose(jnp.concatenate(
        [pos[0].astype(f32), pos[1].astype(f32), jnp.zeros((128 - 2 * SR, 128), f32)], axis=0))
    blocks, offc = [jnp.concatenate([both[:, k:k + 1] for k in range(b, b + SR)], axis=0) for b in (0, SR)]
    lane = lax.broadcasted_iota(jnp.int32, (S, 128), 1)
    onehot = (blocks == lane.astype(f32)).astype(f32)
    ri = lax.broadcasted_iota(jnp.int32, (S, S), 0)
    ci = lax.broadcasted_iota(jnp.int32, (S, S), 1)
    before = jnp.dot((ci < ri).astype(bf16), onehot.astype(bf16), preferred_element_type=f32)
    slot = jnp.sum(before * onehot, axis=1, keepdims=True)
    val = jnp.where(lane.astype(f32) == slot, offc - float(rows), 0.0)
    wanted = lax.dot_general(onehot, val, TN, precision=HI, preferred_element_type=f32) + float(rows)
    wanted = wanted.astype(jnp.int32)
    for j in range(D):
        req[j // Z, j % Z] = wanted[j:j + 1, :]
    place = blocks * float(cap) + slot
    for k in range(S // 128):
        t = jnp.transpose(jnp.broadcast_to(place[k * 128:(k + 1) * 128, :], (128, 128)))
        own[k] = t[0:1, :].astype(jnp.int32)
    oc = pltpu.make_async_copy(own, owns, l_sem.at[0])
    oc.start()

    for j in xpeers:
        c_rx(j).start()
    reqx[mx] = req[mx]
    for j in xpeers:
        w_rx(j).wait_recv()
    for k in range(1, Z):
        c_rz(zpeers(k)).start()
    reqr[:, mz] = reqx[:, mz]
    recv[pl.ds(pl.multiple_of(me * rb, rb), rb), :] = v[pl.ds(pl.multiple_of(me * rb, rb), rb), :]
    table[rows:rows + 8, :] = jnp.zeros((8, W), f32)
    for k in range(1, Z):
        w_rz(zpeers(k)).wait_recv()
    rc = pltpu.make_async_copy(reqr, reqs, l_sem.at[1])
    rc.start()
    rc.wait()
    oc.wait()
    all_sec.wait_recv()

    lowb = rb.bit_length() - 1
    left, low, first = D.bit_length() - 1, lowb, True
    while left:
        b = min(3, left)
        left -= b
        mix_pass(recv if first else table, table, rows, low, b, norm if left == 0 else None)
        low, first = low + b, False

    R = D * cap
    for x in range(X):
        def answer(z, _, x=x):
            for c in range(cap):
                ans[x, pl.ds(z * cap + c, 1), :] = table[pl.ds(jnp.clip(reqs[x, z, 0, c], 0, rows), 1), :]
            return 0
        lax.fori_loop(0, Z, answer, 0, unroll=2 if Z % 2 == 0 else 1)
        xall[col, x * Z * cap:(x + 1) * Z * cap, :] = ans[x]

    half = R // 2
    up, down = lax.rem(col + 2, C), lax.rem(col + C - 2, C)

    def c_col(s, h, t):
        ref = xall.at[s, pl.ds(h * half, half), :]
        return rcopy(ref, ref, s_col.at[s, h, t], r_col.at[s, h], c=(sib, up, down)[t])
    started = []

    def go(s, h, t):
        started.append(c_col(s, h, t))
        started[-1].start()
    ring = C > 4
    far = lax.rem(col + 4, C)
    go(col, 0, 2)
    go(col, 1, 1 if ring else 2)
    go(col, 0, 0)
    go(col, 1, 0)
    if ring:
        go(col, 1, 2)
        go(col, 0, 1)
    slots = lambda ref, z: ref.at[:, pl.ds(pl.multiple_of(z * cap, 8), cap), :]
    c_az = lambda j: rcopy(slots(ans, j), slots(ansz, mz), s_az.at[j], r_az.at[mz], row=mx * Z + j)
    w_az = lambda j: rcopy(slots(ans, j), slots(ansz, j), s_az.at[j], r_az.at[j], row=mx * Z + j)
    flat = lambda x: ret.at[pl.ds(pl.multiple_of(x * Z * cap, 8), Z * cap), :]
    c_ax = lambda j: rcopy(ansz.at[j], flat(mx), s_ax.at[j], r_ax.at[mx], row=j * Z + mz)
    w_ax = lambda j: rcopy(ansz.at[j], flat(j), s_ax.at[j], r_ax.at[j], row=j * Z + mz)

    mine = jnp.transpose(xall[col])

    def block(s):
        part[pl.ds(pl.multiple_of(s * W, W), W), :] = jnp.transpose(
            jnp.dot(mine, xall[s], precision=HI, preferred_element_type=f32))
    block(col)
    if ring:
        c_col(up, 0, 0).wait_recv()
        go(up, 0, 2)
        go(up, 0, 0)
        c_col(down, 1, 0).wait_recv()
        go(down, 1, 1)
        go(down, 1, 0)
    if ring:
        c_col(up, 1, 0).wait_recv()
        go(up, 1, 0)
        block(up)
        c_col(down, 0, 0).wait_recv()
        go(down, 0, 0)
        block(down)
        for h in range(2):
            c_col(far, h, 0).wait_recv()
            go(far, h, 0)
        block(far)
    else:
        for h in range(2):
            c_col(up, h, 0).wait_recv()
            go(up, h, 0)
        block(up)
    for k in (0, 1, 3, 2) if ring else (0, 1):
        s = lax.rem(sib + 2 * k, C)
        for h in range(2):
            c_col(s, h, 0).wait_recv()
        block(s)

    q = C * W // X
    xs = lambda j: part.at[pl.ds(pl.multiple_of(j * q, q), q), :]
    c_x = lambda j: rcopy(xs(j), xr.at[mx], s_x.at[j], r_x.at[mx], row=j * Z + mz)
    w_x = lambda j: rcopy(xs(j), xr.at[j], s_x.at[j], r_x.at[j], row=j * Z + mz)
    for j in xpeers:
        c_x(j).start()
    xr[mx] = part[pl.ds(pl.multiple_of(mx * q, q), q), :]

    for j in xpeers:
        w_x(j).wait_recv()
    acc = xr[0]
    for j in range(1, X):
        acc = acc + xr[j]
    e = q // Z
    zs[...] = acc.reshape(Z, e, W)
    c_z = lambda j: rcopy(zs.at[j], zr.at[mz], s_z.at[j], r_z.at[mz], row=mx * Z + j)
    w_z = lambda j: rcopy(zs.at[j], zr.at[j], s_z.at[j], r_z.at[j], row=mx * Z + j)
    for k in range(1, Z):
        c_z(zpeers(k)).start()
    zr[mz] = zs[mz]
    for k in range(1, Z):
        w_z(zpeers(k)).wait_recv()
    acc = zr[0]
    for j in range(1, Z):
        acc = acc + zr[j]
    gb[col, pl.ds(pl.multiple_of(mx * q + mz * e, e), e), :] = acc / samples
    ze = lambda j: gb.at[col, pl.ds(pl.multiple_of(mx * q + j * e, e), e), :]
    c_zg = lambda j: rcopy(ze(mz), ze(mz), s_zg.at[j], r_zg.at[mz], row=mx * Z + j)
    w_zg = lambda j: rcopy(ze(j), ze(j), s_zg.at[j], r_zg.at[j], row=mx * Z + j)
    for k in range(1, Z):
        c_zg(zpeers(k)).start()
    for k in range(1, Z):
        w_zg(zpeers(k)).wait_recv()
    per = C // X
    gblk = lambda s, p: gb.at[s, pl.ds(pl.multiple_of(p * W, W), W), :]
    c_xg = lambda p, j: rcopy(gblk(col, p), gblk(col, p), s_xg.at[p, j], r_xg.at[p], row=j * Z + mz)
    c_cg = lambda p, k: rcopy(gblk(col, p), gblk(col, p), s_cg.at[p, k], r_cg.at[col, p], c=(up, down)[k])
    c_fw = lambda s, p: rcopy(gblk(s, p), gblk(s, p), s_fw.at[s, p], r_cg.at[s, p], c=sib)
    c_rl = lambda s, p, k: rcopy(gblk(s, p), gblk(s, p), s_rl.at[p], r_cg.at[s, p], c=(up, down)[k])
    sides = [(up, 1), (down, 0)] if ring else [(up, 1)]

    def along_x(p):
        @pl.when((mx == p // per) & (p <= col))
        def _():
            for j in xpeers:
                c_xg(p, j).start()

    def own_block(p):
        @pl.when(p <= col)
        def _():
            @pl.when(mx != p // per)
            def _():
                c_xg(p, mx).wait_recv()
            for k in range(len(sides)):
                c_cg(p, k).start()
            c_fw(col, p).start()

    def relayed(p, do):
        for b, (s, k) in enumerate(sides):
            @pl.when(p <= s)
            def _():
                do(s, p, k, b)

    def relay(p):
        def do(s, p, k, b):
            c_fw(s, p).wait_recv()
            if ring:
                @pl.when(p % 2 == b)
                def _():
                    c_rl(s, p, k).start()
            c_fw(s, p).start()
        relayed(p, do)

    def opposite(p):
        if ring:
            @pl.when(p <= far)
            def _():
                c_fw(far, p).wait_recv()
                c_fw(far, p).start()

    def arrived(p):
        for k in range(C // 2):
            s = lax.rem(sib + 2 * k, C)

            @pl.when(p <= s)
            def _():
                c_fw(s, p).wait_recv()

    def each(fn, lo, hi):
        lax.fori_loop(lo, hi, lambda p, _: (fn(p), 0)[1], 0)
    each(along_x, 0, C)
    own_block(0)
    own_block(1)
    u[...] = jnp.zeros_like(u)
    relay(0)
    own_block(2)
    relay(1)
    opposite(0)

    pr = lax.broadcasted_iota(jnp.int32, (W, W), 0)
    pc = lax.broadcasted_iota(jnp.int32, (W, W), 1)

    def panel(p, _):
        for ahead, fn in ((3, own_block), (2, relay), (1, opposite)):
            @pl.when(p + ahead < C)
            def _():
                fn(p + ahead)
        arrived(p)
        base = pl.multiple_of(p * W, W)
        for pp in range(C):
            @pl.when(p == pp)
            def _():
                a0 = pp * W
                for t in range(pp, C):
                    u[a0:a0 + W, t * W:(t + 1) * W] = gb[t, a0:a0 + W, :]
                if pp:
                    u[a0:a0 + W, a0:] = u[a0:a0 + W, a0:] - lax.dot_general(
                        u[0:a0, a0:a0 + W], u[0:a0, a0:], TN, precision=HI, preferred_element_type=f32)
        aug[:, 0:W] = u[pl.ds(base, W), pl.ds(base, W)]
        aug[:, W:] = jnp.where(pr == pc, 1.0, 0.0).astype(f32)
        panel_factor(aug, upan)
        u[pl.ds(base, W), pl.ds(base, W)] = jnp.where(pr <= pc, upan[:, 0:W], 0.0)
        for pp in range(C - 1):
            @pl.when(p == pp)
            def _():
                a0, a1 = pp * W, (pp + 1) * W
                linv = jnp.where(pr >= pc, upan[:, W:], 0.0)
                u[a0:a1, a1:] = jnp.dot(linv, u[a0:a1, a1:], precision=HI, preferred_element_type=f32)

        @pl.when(p == 0)
        def _():
            for k in range(1, Z):
                c_az(zpeers(k)).start()
            ansz[:, pl.ds(pl.multiple_of(mz * cap, 8), cap), :] = ans[:, pl.ds(pl.multiple_of(mz * cap, 8), cap), :]

        @pl.when(p == C // 2)
        def _():
            for k in range(1, Z):
                w_az(zpeers(k)).wait_recv()
            for j in xpeers:
                c_ax(j).start()
            ret[pl.ds(pl.multiple_of(mx * Z * cap, 8), Z * cap), :] = ansz[mx]

        @pl.when(p == C - 2)
        def _():
            for j in xpeers:
                w_ax(j).wait_recv()

            def keep(t, _):
                k, first = t // 16, t % 16
                for i in range(8):
                    at = jnp.clip(owns[k, 0, first * 8 + i], 0, R - 1)
                    sk_ref[pl.ds(t * 8 + i, 1), :] = ret[pl.ds(at, 1), :]
                return 0
            lax.fori_loop(0, S // 8, keep, 0)
        return 0

    lax.fori_loop(0, C, panel, 0)
    here = pl.ds(pl.multiple_of(col * W, W), W)
    for j in range(C):
        fac_ref[j * W:(j + 1) * W, :] = jnp.transpose(u[here, j * W:(j + 1) * W])

    all_sec.wait_send()
    for j in xpeers:
        w_rx(j).wait_send()
        w_ax(j).wait_send()
    for k in range(1, Z):
        w_rz(zpeers(k)).wait_send()
        w_az(zpeers(k)).wait_send()
    for c in started:
        c.wait_send()
    for j in xpeers:
        w_x(j).wait_send()

    def left(p):
        @pl.when(p <= col)
        def _():
            @pl.when(mx == p // per)
            def _():
                for j in xpeers:
                    c_xg(p, j).wait_send()
            for k in range(len(sides)):
                c_cg(p, k).wait_send()
            c_fw(col, p).wait_send()

        def do(s, p, k, b):
            if ring:
                @pl.when(p % 2 == b)
                def _():
                    c_rl(s, p, k).wait_send()
            c_fw(s, p).wait_send()
        relayed(p, do)
        if ring:
            @pl.when(p <= far)
            def _():
                c_fw(far, p).wait_send()
    each(left, 0, C)
    for k in range(1, Z):
        w_z(zpeers(k)).wait_send()
        w_zg(zpeers(k)).wait_send()


def exchange(a, signs, blocks, offs, X, Z, C):
    rows, W = a.shape
    D = X * Z
    S = offs.shape[0]
    cap = max(2, 2 * S // D)
    rb = rows // D
    R = D * cap
    q = C * W // X
    V = pltpu.VMEM
    dma = pltpu.SemaphoreType.DMA
    return pl.pallas_call(
        functools.partial(exchange_kernel, X, Z, C, 1.0 / math.sqrt(D * rows), float(D * S)),
        out_shape=(jax.ShapeDtypeStruct((C * W, W), f32), jax.ShapeDtypeStruct((S, W), f32)),
        in_specs=[pl.BlockSpec(memory_space=pl.ANY)] * 4,
        out_specs=(pl.BlockSpec(memory_space=V), pl.BlockSpec(memory_space=V)),
        scratch_shapes=[
            V((rows, W), f32), V((rows // 128, 128), jnp.int32), V((2, S // 128, 128), jnp.int32),
            V((rows, W), f32), V((rows + 8, W), f32),
            V((X, Z, 1, 128), jnp.int32), V((X, Z, 1, 128), jnp.int32), V((X, Z, 1, 128), jnp.int32),
            pltpu.SMEM((X, Z, 1, 128), jnp.int32),
            V((S // 128, 1, 128), jnp.int32), pltpu.SMEM((S // 128, 1, 128), jnp.int32),
            V((X, Z * cap, W), f32), V((X, Z * cap, W), f32), V((R, W), f32), V((C, R, W), f32),
            V((C * W, W), f32), V((X, q, W), f32), V((Z, q // Z, W), f32), V((Z, q // Z, W), f32),
            V((C, C * W, W), f32), V((C * W, C * W), f32), V((W, 2 * W), f32), V((W, 2 * W), f32),
            dma((X,)), dma((X,)), dma((Z,)), dma((Z,)), dma((1,)), dma((1,)), dma((Z,)), dma((Z,)), dma((X,)), dma((X,)),
            dma((C, 2, 3)), dma((C, 2)), dma((X,)), dma((X,)), dma((Z,)), dma((Z,)),
            dma((Z,)), dma((Z,)), dma((C, X)), dma((C,)), dma((C, 2)), dma((C, C)), dma((C,)), dma((C, C)), dma((6,)),
        ],
        compiler_params=pltpu.CompilerParams(collective_id=0, has_side_effects=True, vmem_limit_bytes=60 * 2**20),
        name="exchange",
    )(a, signs.reshape(rows // 128, 128), blocks.reshape(S // 128, 128), offs.reshape(S // 128, 128))


def solution(mesh):
    x_size, z_size, c_size = 4, mesh.shape["row"] // 4, mesh.shape["col"]

    def shards(matrix, row_signs, sample_block, sample_offset):
        factor, sketch = exchange(matrix, row_signs, sample_block, sample_offset, x_size, z_size, c_size)
        return sketch, factor

    placed = (P("row", "col"), P("row"), P("row", None), P("row"))
    return jax.shard_map(
        shards,
        mesh=mesh,
        in_specs=placed,
        out_specs=(P("row", "col"), P(None, "col")),
        check_vma=False,
    )
```

time: 169 us -> 168 us (level); the launches traced: 166 us -> 167 us
  Pallas kernels: 161 us -> 163 us
    pallas_call x1, Pallas kernels: 161 us -> 163 us  [exchange(): pl.pallas_call(functools.partial(exchange_kernel, X, Z, C, 1.0 / math.sqr...]
    unnamed x11 -> x2, local copies, waits for them, and re-layouts: 4.04 us -> 3.44 us
where the time goes in v4:
time: 168 us; the launch traced here: 167 us
  Pallas kernels  163 us (97%)
  local copies, waits for them, and re-layouts  3.44 us (2%)
    pallas_call x1, Pallas kernels, exchange(): pl.pallas_call(functools.partial(exchange_kernel, X, Z, C, 1.0 / math.sqr...  163 us
    unnamed x2, local copies, waits for them, and re-layouts  3.44 us

profile of v4, /device:TPU:1, one launch (start us, length us, event | category | flops | bytes accessed | tf_op | source)
XLA Modules:
  0.0 167.4 jit_solution(17853085597995946262)
XLA Ops:
  0.6 163.3 %exchange.1 = (f32[1024,128]{1,0:T(8,128)}, f32[256,128]{1,0:T(8,128)}) custom-call(f32[2048,128]{1,0:T(8,128)} %a_ref.1, s32[16,128]{1,0:T(8,128)} %bitcast.3, s32[2,128]{1,0:T(2,128)} %bitcast.4, s32[2,128]{1,0:T(2,128)} %bitcast.5), custom_call_target="tpu_custom_call" | custom-call | tf_op jit(solution)/shard_map/exchange/pallas_call | solution.py:501
  164.0 1.6 copy.8
  165.6 1.9 %copy.9 = f32[1024,128]{1,0:T(8,128)} copy(f32[1024,128]{1,0:T(8,128)} %get-tuple-element.9) | data formatting | bytes 1048576

commit v5 on v4

--- a/solution.py
+++ b/solution.py
@@ -92,7 +92,7 @@
                     v, sign, pos, recv, table, req, reqx, reqr, reqs, own, owns, ans, ansz, ret, xall, part, xr, zs, zr,
                     gb, u, aug, upan,
                     s_rx, r_rx, s_rz, r_rz, s_sec, r_sec, s_az, r_az, s_ax, r_ax, s_col, r_col, s_x, r_x, s_z, r_z,
-                    s_zg, r_zg, s_xg, r_xg, s_cg, s_fw, s_rl, r_cg, l_sem):
+                    s_zg, r_zg, s_xg, r_xg, s_cg, s_fw, r_cg, l_sem):
     D = X * Z
     rows, W = v.shape
     rb = rows // D
@@ -147,11 +147,11 @@
     def peer_of(k):
         return lax.rem(me + jnp.where(k % 2 == 1, (k + 1) // 2, D - k // 2), D)
 
-    def sends(fn):
+    def sends(fn, lo, hi):
         def go(k, _):
             fn(peer_of(k)).start()
             return 0
-        lax.fori_loop(1, D, go, 0)
+        lax.fori_loop(lo, hi, go, 0)
 
     xpeers = [lax.rem(mx + k, X) for k in range(1, X)]
     zpeers = lambda k: lax.rem(mz + k, Z)
@@ -164,7 +164,7 @@
     c_sec = lambda j: rcopy(sec(j), got(me), s_sec.at[0], r_sec.at[0], row=j)
     others = pl.ds(0, (D - 1) * rb)
     all_sec = rcopy(v.at[others, :], recv.at[others, :], s_sec.at[0], r_sec.at[0], row=lax.rem(me + 1, D))
-    sends(c_sec)
+    sends(c_sec, 1, D // 4)
     fetch[0].wait()
     fetch[1].wait()
 
@@ -192,10 +192,12 @@
     for j in xpeers:
         c_rx(j).start()
     reqx[mx] = req[mx]
+    sends(c_sec, D // 4, D // 2)
     for j in xpeers:
         w_rx(j).wait_recv()
     for k in range(1, Z):
         c_rz(zpeers(k)).start()
+    sends(c_sec, D // 2, D)
     reqr[:, mz] = reqx[:, mz]
     recv[pl.ds(pl.multiple_of(me * rb, rb), rb), :] = v[pl.ds(pl.multiple_of(me * rb, rb), rb), :]
     table[rows:rows + 8, :] = jnp.zeros((8, W), f32)
@@ -256,42 +258,49 @@
     def block(s):
         part[pl.ds(pl.multiple_of(s * W, W), W), :] = jnp.transpose(
             jnp.dot(mine, xall[s], precision=HI, preferred_element_type=f32))
-    block(col)
+    q = C * W // X
+    xs = lambda j: part.at[pl.ds(pl.multiple_of(j * q, q), q), :]
+    c_x = lambda j: rcopy(xs(j), xr.at[mx], s_x.at[j], r_x.at[mx], row=j * Z + mz)
+    w_x = lambda j: rcopy(xs(j), xr.at[j], s_x.at[j], r_x.at[j], row=j * Z + mz)
+    per_x = X * 2 // C
+    chip = col // 2
+
+    def along(k):
+        a, b = lax.rem(col + 2 * k, C), lax.rem(sib + 2 * k, C)
+        for h in range(2):
+            c_col(b, h, 0).wait_recv()
+        block(a)
+        block(b)
+        j = lax.rem(chip + k, C // 2)
+        for n in range(per_x):
+            @pl.when(mx != j * per_x + n)
+            def _():
+                c_x(j * per_x + n).start()
     if ring:
+        along(0)
         c_col(up, 0, 0).wait_recv()
         go(up, 0, 2)
         go(up, 0, 0)
         c_col(down, 1, 0).wait_recv()
         go(down, 1, 1)
         go(down, 1, 0)
-    if ring:
         c_col(up, 1, 0).wait_recv()
         go(up, 1, 0)
-        block(up)
         c_col(down, 0, 0).wait_recv()
         go(down, 0, 0)
-        block(down)
+        along(1)
+        along(3)
         for h in range(2):
             c_col(far, h, 0).wait_recv()
             go(far, h, 0)
-        block(far)
+        along(2)
     else:
         for h in range(2):
             c_col(up, h, 0).wait_recv()
             go(up, h, 0)
-        block(up)
-    for k in (0, 1, 3, 2) if ring else (0, 1):
-        s = lax.rem(sib + 2 * k, C)
-        for h in range(2):
-            c_col(s, h, 0).wait_recv()
-        block(s)
-
-    q = C * W // X
-    xs = lambda j: part.at[pl.ds(pl.multiple_of(j * q, q), q), :]
-    c_x = lambda j: rcopy(xs(j), xr.at[mx], s_x.at[j], r_x.at[mx], row=j * Z + mz)
-    w_x = lambda j: rcopy(xs(j), xr.at[j], s_x.at[j], r_x.at[j], row=j * Z + mz)
-    for j in xpeers:
-        c_x(j).start()
+        along(0)
+        along(1)
+
     xr[mx] = part[pl.ds(pl.multiple_of(mx * q, q), q), :]
 
     for j in xpeers:
@@ -318,14 +327,15 @@
     for k in range(1, Z):
         c_zg(zpeers(k)).start()
     for k in range(1, Z):
+        c_az(zpeers(k)).start()
+    ansz[:, pl.ds(pl.multiple_of(mz * cap, 8), cap), :] = ans[:, pl.ds(pl.multiple_of(mz * cap, 8), cap), :]
+    for k in range(1, Z):
         w_zg(zpeers(k)).wait_recv()
     per = C // X
     gblk = lambda s, p: gb.at[s, pl.ds(pl.multiple_of(p * W, W), W), :]
     c_xg = lambda p, j: rcopy(gblk(col, p), gblk(col, p), s_xg.at[p, j], r_xg.at[p], row=j * Z + mz)
-    c_cg = lambda p, k: rcopy(gblk(col, p), gblk(col, p), s_cg.at[p, k], r_cg.at[col, p], c=(up, down)[k])
+    c_cg = lambda p, k: rcopy(gblk(col, p), gblk(col, p), s_cg.at[p, k], r_cg.at[col, p], c=ypeers[k])
     c_fw = lambda s, p: rcopy(gblk(s, p), gblk(s, p), s_fw.at[s, p], r_cg.at[s, p], c=sib)
-    c_rl = lambda s, p, k: rcopy(gblk(s, p), gblk(s, p), s_rl.at[p], r_cg.at[s, p], c=(up, down)[k])
-    sides = [(up, 1), (down, 0)] if ring else [(up, 1)]
 
     def along_x(p):
         @pl.when((mx == p // per) & (p <= col))
@@ -339,32 +349,16 @@
             @pl.when(mx != p // per)
             def _():
                 c_xg(p, mx).wait_recv()
-            for k in range(len(sides)):
+            c_fw(col, p).start()
+            for k in (1, 0, 2) if len(ypeers) == 3 else range(len(ypeers)):
                 c_cg(p, k).start()
-            c_fw(col, p).start()
-
-    def relayed(p, do):
-        for b, (s, k) in enumerate(sides):
+
+    def pass_on(p):
+        for s in ypeers:
             @pl.when(p <= s)
             def _():
-                do(s, p, k, b)
-
-    def relay(p):
-        def do(s, p, k, b):
-            c_fw(s, p).wait_recv()
-            if ring:
-                @pl.when(p % 2 == b)
-                def _():
-                    c_rl(s, p, k).start()
-            c_fw(s, p).start()
-        relayed(p, do)
-
-    def opposite(p):
-        if ring:
-            @pl.when(p <= far)
-            def _():
-                c_fw(far, p).wait_recv()
-                c_fw(far, p).start()
+                c_fw(s, p).wait_recv()
+                c_fw(s, p).start()
 
     def arrived(p):
         for k in range(C // 2):
@@ -380,16 +374,14 @@
     own_block(0)
     own_block(1)
     u[...] = jnp.zeros_like(u)
-    relay(0)
     own_block(2)
-    relay(1)
-    opposite(0)
+    pass_on(0)
 
     pr = lax.broadcasted_iota(jnp.int32, (W, W), 0)
     pc = lax.broadcasted_iota(jnp.int32, (W, W), 1)
 
     def panel(p, _):
-        for ahead, fn in ((3, own_block), (2, relay), (1, opposite)):
+        for ahead, fn in ((3, own_block), (1, pass_on)):
             @pl.when(p + ahead < C)
             def _():
                 fn(p + ahead)
@@ -415,12 +407,6 @@
                 linv = jnp.where(pr >= pc, upan[:, W:], 0.0)
                 u[a0:a1, a1:] = jnp.dot(linv, u[a0:a1, a1:], precision=HI, preferred_element_type=f32)
 
-        @pl.when(p == 0)
-        def _():
-            for k in range(1, Z):
-                c_az(zpeers(k)).start()
-            ansz[:, pl.ds(pl.multiple_of(mz * cap, 8), cap), :] = ans[:, pl.ds(pl.multiple_of(mz * cap, 8), cap), :]
-
         @pl.when(p == C // 2)
         def _():
             for k in range(1, Z):
@@ -467,21 +453,13 @@
             def _():
                 for j in xpeers:
                     c_xg(p, j).wait_send()
-            for k in range(len(sides)):
+            for k in range(len(ypeers)):
                 c_cg(p, k).wait_send()
             c_fw(col, p).wait_send()
-
-        def do(s, p, k, b):
-            if ring:
-                @pl.when(p % 2 == b)
-                def _():
-                    c_rl(s, p, k).wait_send()
-            c_fw(s, p).wait_send()
-        relayed(p, do)
-        if ring:
-            @pl.when(p <= far)
-            def _():
-                c_fw(far, p).wait_send()
+        for s in ypeers:
+            @pl.when(p <= s)
+            def _():
+                c_fw(s, p).wait_send()
     each(left, 0, C)
     for k in range(1, Z):
         w_z(zpeers(k)).wait_send()
@@ -514,7 +492,7 @@
             V((C, C * W, W), f32), V((C * W, C * W), f32), V((W, 2 * W), f32), V((W, 2 * W), f32),
             dma((X,)), dma((X,)), dma((Z,)), dma((Z,)), dma((1,)), dma((1,)), dma((Z,)), dma((Z,)), dma((X,)), dma((X,)),
             dma((C, 2, 3)), dma((C, 2)), dma((X,)), dma((X,)), dma((Z,)), dma((Z,)),
-            dma((Z,)), dma((Z,)), dma((C, X)), dma((C,)), dma((C, 2)), dma((C, C)), dma((C,)), dma((C, C)), dma((6,)),
+            dma((Z,)), dma((Z,)), dma((C, X)), dma((C,)), dma((C, C // 2)), dma((C, C)), dma((C, C)), dma((6,)),
         ],
         compiler_params=pltpu.CompilerParams(collective_id=0, has_side_effects=True, vmem_limit_bytes=60 * 2**20),
         name="exchange",

time: 168 us -> 163 us (0.970)
  Pallas kernels: 163 us -> 158 us
    pallas_call x1, Pallas kernels: 163 us -> 158 us  [exchange(): pl.pallas_call(functools.partial(exchange_kernel, X, Z, C, 1.0 / math.sqr...]
where the time goes in v5:
time: 163 us; the launch traced here: 162 us
  Pallas kernels  158 us (97%)
  local copies, waits for them, and re-layouts  3.44 us (2%)
    pallas_call x1, Pallas kernels, exchange(): pl.pallas_call(functools.partial(exchange_kernel, X, Z, C, 1.0 / math.sqr...  158 us
    unnamed x2, local copies, waits for them, and re-layouts  3.44 us

profile of v5, /device:TPU:1, one launch (start us, length us, event | category | flops | bytes accessed | tf_op | source)
XLA Modules:
  0.0 162.1 jit_solution(9173171434923592682)
XLA Ops:
  0.6 158.0 %exchange.1 = (f32[1024,128]{1,0:T(8,128)}, f32[256,128]{1,0:T(8,128)}) custom-call(f32[2048,128]{1,0:T(8,128)} %a_ref.1, s32[16,128]{1,0:T(8,128)} %bitcast.3, s32[2,128]{1,0:T(2,128)} %bitcast.4, s32[2,128]{1,0:T(2,128)} %bitcast.5), custom_call_target="tpu_custom_call" | custom-call | tf_op jit(solution)/shard_map/exchange/pallas_call | solution.py:479
  158.7 1.6 copy.8
  160.3 1.9 %copy.9 = f32[1024,128]{1,0:T(8,128)} copy(f32[1024,128]{1,0:T(8,128)} %get-tuple-element.9) | data formatting | bytes 1048576

commit v6 on v5

--- a/solution.py
+++ b/solution.py
@@ -86,6 +86,18 @@
             cur = [[nxt[8 * r:8 * r + 8, h * PAN:(h + 1) * PAN] - acc[r][h] for h in range(lanes)] for r in range(sub)]
 
 
+def split2(x):
+    h = x.astype(bf16)
+    return h, (x - h.astype(f32)).astype(bf16)
+
+
+def dot3(a, b):
+    ah, al = split2(a)
+    bh, bl = split2(b)
+    return jnp.dot(jnp.concatenate([ah, al], axis=1), jnp.concatenate([bh, bh], axis=0), preferred_element_type=f32) \
+        + jnp.dot(ah, bl, preferred_element_type=f32)
+
+
 def exchange_kernel(X, Z, C, norm, samples,
                     a_ref, sign_ref, blk_ref, off_ref,
                     fac_ref, sk_ref,
@@ -252,6 +264,9 @@
     flat = lambda x: ret.at[pl.ds(pl.multiple_of(x * Z * cap, 8), Z * cap), :]
     c_ax = lambda j: rcopy(ansz.at[j], flat(mx), s_ax.at[j], r_ax.at[mx], row=j * Z + mz)
     w_ax = lambda j: rcopy(ansz.at[j], flat(j), s_ax.at[j], r_ax.at[j], row=j * Z + mz)
+    for k in range(1, Z):
+        c_az(zpeers(k)).start()
+    ansz[:, pl.ds(pl.multiple_of(mz * cap, 8), cap), :] = ans[:, pl.ds(pl.multiple_of(mz * cap, 8), cap), :]
 
     mine = jnp.transpose(xall[col])
 
@@ -316,6 +331,11 @@
         c_z(zpeers(k)).start()
     zr[mz] = zs[mz]
     for k in range(1, Z):
+        w_az(zpeers(k)).wait_recv()
+    for j in xpeers:
+        c_ax(j).start()
+    ret[pl.ds(pl.multiple_of(mx * Z * cap, 8), Z * cap), :] = ansz[mx]
+    for k in range(1, Z):
         w_z(zpeers(k)).wait_recv()
     acc = zr[0]
     for j in range(1, Z):
@@ -327,9 +347,6 @@
     for k in range(1, Z):
         c_zg(zpeers(k)).start()
     for k in range(1, Z):
-        c_az(zpeers(k)).start()
-    ansz[:, pl.ds(pl.multiple_of(mz * cap, 8), cap), :] = ans[:, pl.ds(pl.multiple_of(mz * cap, 8), cap), :]
-    for k in range(1, Z):
         w_zg(zpeers(k)).wait_recv()
     per = C // X
     gblk = lambda s, p: gb.at[s, pl.ds(pl.multiple_of(p * W, W), W), :]
@@ -374,15 +391,32 @@
     own_block(0)
     own_block(1)
     u[...] = jnp.zeros_like(u)
+    for j in xpeers:
+        w_ax(j).wait_recv()
+
+    def keep(t, _):
+        k, first = t // 16, t % 16
+        for i in range(8):
+            at = jnp.clip(owns[k, 0, first * 8 + i], 0, R - 1)
+            sk_ref[pl.ds(t * 8 + i, 1), :] = ret[pl.ds(at, 1), :]
+        return 0
+    lax.fori_loop(0, S // 8, keep, 0)
+    pass_on(0)
     own_block(2)
-    pass_on(0)
+    all_sec.wait_send()
+    for j in xpeers:
+        w_rx(j).wait_send()
+    for k in range(1, Z):
+        w_rz(zpeers(k)).wait_send()
+        w_az(zpeers(k)).wait_send()
+        w_z(zpeers(k)).wait_send()
 
     pr = lax.broadcasted_iota(jnp.int32, (W, W), 0)
     pc = lax.broadcasted_iota(jnp.int32, (W, W), 1)
 
     def panel(p, _):
         for ahead, fn in ((3, own_block), (1, pass_on)):
-            @pl.when(p + ahead < C)
+            @pl.when((p > 0) & (p + ahead < C))
             def _():
                 fn(p + ahead)
         arrived(p)
@@ -394,39 +428,23 @@
                 for t in range(pp, C):
                     u[a0:a0 + W, t * W:(t + 1) * W] = gb[t, a0:a0 + W, :]
                 if pp:
-                    u[a0:a0 + W, a0:] = u[a0:a0 + W, a0:] - lax.dot_general(
-                        u[0:a0, a0:a0 + W], u[0:a0, a0:], TN, precision=HI, preferred_element_type=f32)
+                    u[a0:a0 + W, a0:] = u[a0:a0 + W, a0:] - dot3(
+                        jnp.transpose(u[0:a0, a0:a0 + W]), u[0:a0, a0:])
         aug[:, 0:W] = u[pl.ds(base, W), pl.ds(base, W)]
         aug[:, W:] = jnp.where(pr == pc, 1.0, 0.0).astype(f32)
         panel_factor(aug, upan)
         u[pl.ds(base, W), pl.ds(base, W)] = jnp.where(pr <= pc, upan[:, 0:W], 0.0)
+
+        @pl.when(p == 0)
+        def _():
+            own_block(3)
+            pass_on(1)
         for pp in range(C - 1):
             @pl.when(p == pp)
             def _():
                 a0, a1 = pp * W, (pp + 1) * W
                 linv = jnp.where(pr >= pc, upan[:, W:], 0.0)
-                u[a0:a1, a1:] = jnp.dot(linv, u[a0:a1, a1:], precision=HI, preferred_element_type=f32)
-
-        @pl.when(p == C // 2)
-        def _():
-            for k in range(1, Z):
-                w_az(zpeers(k)).wait_recv()
-            for j in xpeers:
-                c_ax(j).start()
-            ret[pl.ds(pl.multiple_of(mx * Z * cap, 8), Z * cap), :] = ansz[mx]
-
-        @pl.when(p == C - 2)
-        def _():
-            for j in xpeers:
-                w_ax(j).wait_recv()
-
-            def keep(t, _):
-                k, first = t // 16, t % 16
-                for i in range(8):
-                    at = jnp.clip(owns[k, 0, first * 8 + i], 0, R - 1)
-                    sk_ref[pl.ds(t * 8 + i, 1), :] = ret[pl.ds(at, 1), :]
-                return 0
-            lax.fori_loop(0, S // 8, keep, 0)
+                u[a0:a1, a1:] = dot3(linv, u[a0:a1, a1:])
         return 0
 
     lax.fori_loop(0, C, panel, 0)
@@ -434,13 +452,8 @@
     for j in range(C):
         fac_ref[j * W:(j + 1) * W, :] = jnp.transpose(u[here, j * W:(j + 1) * W])
 
-    all_sec.wait_send()
-    for j in xpeers:
-        w_rx(j).wait_send()
+    for j in xpeers:
         w_ax(j).wait_send()
-    for k in range(1, Z):
-        w_rz(zpeers(k)).wait_send()
-        w_az(zpeers(k)).wait_send()
     for c in started:
         c.wait_send()
     for j in xpeers:
@@ -462,7 +475,6 @@
                 c_fw(s, p).wait_send()
     each(left, 0, C)
     for k in range(1, Z):
-        w_z(zpeers(k)).wait_send()
         w_zg(zpeers(k)).wait_send()
 
 

time: 163 us -> 157 us (0.963)
  Pallas kernels: 158 us -> 150 us
    pallas_call x1, Pallas kernels: 158 us -> 150 us  [exchange(): pl.pallas_call(functools.partial(exchange_kernel, X, Z, C, 1.0 / math.sqr...]
where the time goes in v6:
time: 157 us; the launch traced here: 155 us
  Pallas kernels  150 us (96%)
  local copies, waits for them, and re-layouts  3.44 us (2%)
    pallas_call x1, Pallas kernels, exchange(): pl.pallas_call(functools.partial(exchange_kernel, X, Z, C, 1.0 / math.sqr...  150 us
    unnamed x2, local copies, waits for them, and re-layouts  3.44 us

profile of v6, /device:TPU:1, one launch (start us, length us, event | category | flops | bytes accessed | tf_op | source)
XLA Modules:
  0.0 154.6 jit_solution(8093673204486970054)
XLA Ops:
  0.6 150.5 %exchange.1 = (f32[1024,128]{1,0:T(8,128)}, f32[256,128]{1,0:T(8,128)}) custom-call(f32[2048,128]{1,0:T(8,128)} %a_ref.1, s32[16,128]{1,0:T(8,128)} %bitcast.3, s32[2,128]{1,0:T(2,128)} %bitcast.4, s32[2,128]{1,0:T(2,128)} %bitcast.5), custom_call_target="tpu_custom_call" | custom-call | tf_op jit(solution)/shard_map/exchange/pallas_call | solution.py:491
  151.1 1.6 %copy.8 = f32[256,128]{1,0:T(8,128)} copy(f32[256,128]{1,0:T(8,128)} %get-tuple-element.8) | data formatting | bytes 262144
  152.7 1.9 %copy.9 = f32[1024,128]{1,0:T(8,128)} copy(f32[1024,128]{1,0:T(8,128)} %get-tuple-element.9) | data formatting | bytes 1048576

commit v7 on v6

--- a/solution.py
+++ b/solution.py
@@ -150,7 +150,7 @@
     lax.fori_loop(0, rows // 64, low_bits, 0, unroll=2)
     left, low = rows.bit_length() - 1 - 3, 3
     while left:
-        b = min(3, left)
+        b = left if left <= 5 else 3
         mix_pass(v, v, rows, low, b)
         low, left = low + b, left - b
 
@@ -372,16 +372,26 @@
 
     def pass_on(p):
         for s in ypeers:
-            @pl.when(p <= s)
+            @pl.when((p <= s) & (p + s > 0))
             def _():
                 c_fw(s, p).wait_recv()
                 c_fw(s, p).start()
+
+    def first_block():
+        @pl.when((col % 2 == 0) & (col > 0))
+        def _():
+            c_fw(0, 0).wait_recv()
+            c_fw(0, 0).start()
+
+        @pl.when(col % 2 == 1)
+        def _():
+            c_fw(0, 0).wait_recv()
 
     def arrived(p):
         for k in range(C // 2):
             s = lax.rem(sib + 2 * k, C)
 
-            @pl.when(p <= s)
+            @pl.when((p <= s) & (p + s > 0))
             def _():
                 c_fw(s, p).wait_recv()
 
@@ -391,6 +401,13 @@
     own_block(0)
     own_block(1)
     u[...] = jnp.zeros_like(u)
+    all_sec.wait_send()
+    for j in xpeers:
+        w_rx(j).wait_send()
+    for k in range(1, Z):
+        w_rz(zpeers(k)).wait_send()
+        w_az(zpeers(k)).wait_send()
+        w_z(zpeers(k)).wait_send()
     for j in xpeers:
         w_ax(j).wait_recv()
 
@@ -401,15 +418,8 @@
             sk_ref[pl.ds(t * 8 + i, 1), :] = ret[pl.ds(at, 1), :]
         return 0
     lax.fori_loop(0, S // 8, keep, 0)
-    pass_on(0)
     own_block(2)
-    all_sec.wait_send()
-    for j in xpeers:
-        w_rx(j).wait_send()
-    for k in range(1, Z):
-        w_rz(zpeers(k)).wait_send()
-        w_az(zpeers(k)).wait_send()
-        w_z(zpeers(k)).wait_send()
+    first_block()
 
     pr = lax.broadcasted_iota(jnp.int32, (W, W), 0)
     pc = lax.broadcasted_iota(jnp.int32, (W, W), 1)
@@ -419,13 +429,15 @@
             @pl.when((p > 0) & (p + ahead < C))
             def _():
                 fn(p + ahead)
-        arrived(p)
+        @pl.when(p > 0)
+        def _():
+            arrived(p)
         base = pl.multiple_of(p * W, W)
         for pp in range(C):
             @pl.when(p == pp)
             def _():
                 a0 = pp * W
-                for t in range(pp, C):
+                for t in range(pp, C if pp else 1):
                     u[a0:a0 + W, t * W:(t + 1) * W] = gb[t, a0:a0 + W, :]
                 if pp:
                     u[a0:a0 + W, a0:] = u[a0:a0 + W, a0:] - dot3(
@@ -437,8 +449,12 @@
 
         @pl.when(p == 0)
         def _():
+            pass_on(0)
             own_block(3)
             pass_on(1)
+            arrived(0)
+            for t in range(1, C):
+                u[0:W, t * W:(t + 1) * W] = gb[t, 0:W, :]
         for pp in range(C - 1):
             @pl.when(p == pp)
             def _():

time: 157 us -> 156 us (level)
  the two profiles are of different devices: /device:TPU:1 before, /device:TPU:5 now
where the time goes in v7:
time: 156 us
  Pallas kernels  152 us (97%)
  local copies, waits for them, and re-layouts  3.44 us (2%)
    pallas_call x1, Pallas kernels, exchange(): pl.pallas_call(functools.partial(exchange_kernel, X, Z, C, 1.0 / math.sqr...  152 us
    unnamed x2, local copies, waits for them, and re-layouts  3.44 us

profile of v7, /device:TPU:5, one launch (start us, length us, event | category | flops | bytes accessed | tf_op | source)
XLA Modules:
  0.0 156.1 jit_solution(1655521347186690855)
XLA Ops:
  0.6 152.0 %exchange.1 = (f32[1024,128]{1,0:T(8,128)}, f32[256,128]{1,0:T(8,128)}) custom-call(f32[2048,128]{1,0:T(8,128)} %a_ref.1, s32[16,128]{1,0:T(8,128)} %bitcast.3, s32[2,128]{1,0:T(2,128)} %bitcast.4, s32[2,128]{1,0:T(2,128)} %bitcast.5), custom_call_target="tpu_custom_call" | custom-call | tf_op jit(solution)/shard_map/exchange/pallas_call | solution.py:507
  152.7 1.6 %copy.8 = f32[256,128]{1,0:T(8,128)} copy(f32[256,128]{1,0:T(8,128)} %get-tuple-element.8) | data formatting | bytes 262144
  154.2 1.9 %copy.9 = f32[1024,128]{1,0:T(8,128)} copy(f32[1024,128]{1,0:T(8,128)} %get-tuple-element.9) | data formatting | bytes 1048576

commit v8 on v7

--- a/solution.py
+++ b/solution.py
@@ -52,14 +52,13 @@
         last = t == nblk - 1
         C = [[jnp.broadcast_to(cur[r][0][:, lo + k:lo + k + 1], (8, PAN)) for r in range(sub)] for k in range(BLK)]
         if not last:
-            xt = jnp.transpose(jnp.concatenate([cur[r][0] for r in range(sub)], axis=0))[lo + BLK:lo + 2 * BLK, :]
-            N = [[jnp.broadcast_to(xt[8 * r:8 * r + 8, k:k + 1], (8, PAN)) for r in range(sub)] for k in range(BLK)]
             nxt = aug[lo + BLK:lo + 2 * BLK, :]
             if t > 0:
                 done = upan[0:lo, :]
                 nxt = nxt - lax.dot_general(done[:, lo + BLK:lo + 2 * BLK], done, TN,
                                             precision=HI, preferred_element_type=f32)
             acc = [[None] * lanes for _ in range(sub)]
+            N = [[jnp.broadcast_to(nxt[8 * r:8 * r + 8, lo + k:lo + k + 1], (8, PAN)) for r in range(sub)] for k in range(BLK)]
         R = cur
         for k in range(BLK):
             rs = lax.rsqrt(C[k][k // 8][k % 8:k % 8 + 1, :])
@@ -120,6 +119,11 @@
         return pltpu.make_async_remote_copy(src_ref=src, dst_ref=dst, send_sem=ss, recv_sem=rs,
                                             device_id=dev, device_id_type=pl.DeviceIdType.MESH)
 
+    fetch = [pltpu.make_async_copy(src, dst, l_sem.at[2 + k]) for k, (src, dst) in enumerate(
+        [(blk_ref, pos.at[0]), (off_ref, pos.at[1]), (sign_ref, sign), (a_ref, v)])]
+    for c in fetch:
+        c.start()
+
     bar = pltpu.get_barrier_semaphore()
 
     def greet(k, _):
@@ -130,10 +134,6 @@
     for c in [sib] + ypeers:
         pl.semaphore_signal(bar, inc=1, device_id={"col": c}, device_id_type=pl.DeviceIdType.MESH)
 
-    fetch = [pltpu.make_async_copy(src, dst, l_sem.at[2 + k]) for k, (src, dst) in enumerate(
-        [(blk_ref, pos.at[0]), (off_ref, pos.at[1]), (sign_ref, sign), (a_ref, v)])]
-    for c in fetch:
-        c.start()
     nb = rows // 128
     fetch[2].wait()
     fetch[3].wait()

time: 156 us -> 157 us (level)
  the two profiles are of different devices: /device:TPU:5 before, /device:TPU:69 now
where the time goes in v8:
time: 157 us
  Pallas kernels  153 us (97%)
  local copies, waits for them, and re-layouts  3.44 us (2%)
    pallas_call x1, Pallas kernels, exchange(): pl.pallas_call(functools.partial(exchange_kernel, X, Z, C, 1.0 / math.sqr...  153 us
    unnamed x2, local copies, waits for them, and re-layouts  3.44 us

profile of v8, /device:TPU:69, one launch (start us, length us, event | category | flops | bytes accessed | tf_op | source)
XLA Modules:
  0.0 156.7 jit_solution(420369298400798230)
XLA Ops:
  0.6 152.6 %exchange.1 = (f32[1024,128]{1,0:T(8,128)}, f32[256,128]{1,0:T(8,128)}) custom-call(f32[2048,128]{1,0:T(8,128)} %a_ref.1, s32[16,128]{1,0:T(8,128)} %bitcast.3, s32[2,128]{1,0:T(2,128)} %bitcast.4, s32[2,128]{1,0:T(2,128)} %bitcast.5), custom_call_target="tpu_custom_call" | custom-call | tf_op jit(solution)/shard_map/exchange/pallas_call | solution.py:507
  153.3 1.6 %copy.8 = f32[256,128]{1,0:T(8,128)} copy(f32[256,128]{1,0:T(8,128)} %get-tuple-element.8) | data formatting | bytes 262144
  154.8 1.9 %copy.9 = f32[1024,128]{1,0:T(8,128)} copy(f32[1024,128]{1,0:T(8,128)} %get-tuple-element.9) | data formatting | bytes 1048576
